TPU v7x, 256 devices: a whole 4x4x8 slice. The times are simulated.
256 devices in a mesh: lat: 64 (over y, x, z_hi, core), grp: 4 (over z_lo).
Axes of the slice: x: 4, y: 4, z: 8 (z_hi: 2, z_lo: 4; z = z_hi * 4 + z_lo), core: 2. Of those that a mesh axis runs over, the one named last changes fastest.
Arguments:
- increments: bfloat16 [16384, 4, 16, 128], P(('lat', 'grp')), may hold values from -6 to 6
- band: int32 [16384, 1], P(('lat', 'grp')), may hold values from 0 to 63; in each aligned block of 64 rows (0 to 63, 64 to 127, ...) at most 3 rows name the same one
- tile_index: int32 [16384], P(('lat', 'grp')), may hold values from 0 to 7
- lat_offset: int32 [16384], P(('lat', 'grp')), may hold values from 0 to 12
- lon_shift: int32 [16384], P(('lat', 'grp')), may hold values from -8 to 8
- lat_frac: float32 [16384], P(('lat', 'grp')), may hold values from 0 to 1
- lon_frac: float32 [16384, 128], P(('lat', 'grp')), may hold values from 0 to 1
Outputs:
- source_adjoint: float32 [16, 4, 8192, 128], P('grp', None, 'lat')
Inputs may be any that keep to these rules, and one draw needn't show every extreme that they name: In the rows of one device no band is named more than 3 times, a bound that some block reaches.
All inputs are finite; a program needn't handle non-finite values.
Results may differ from a plain program's by a relative error of at most 0.0045.
Values may be sent and summed in bfloat16 or wider, within the bound.
No kernel may reach another device: no remote copies, remote signals or barrier semaphores. Data moves between devices by JAX's collectives and lax.ppermute only.
A program may use at most 64 MiB of HBM per device.

v0:
```python
import math

import jax
import jax.numpy as jnp
from jax import lax
from jax.sharding import PartitionSpec as P

TL = 16
TILES_DEV = 8


def cut_along(array, dim, size):
    lengths = array.shape
    pieces = array.reshape(*lengths[:dim], size, lengths[dim] // size, *lengths[dim + 1 :])
    return jnp.moveaxis(pieces, dim, 0)


def summed_on_arrival(array, axis, dim):
    size = lax.axis_size(axis)
    pieces = lax.all_to_all(cut_along(array, dim, size), axis, 0, 0, tiled=True)
    return jnp.sum(pieces, axis=0)


def lagrange(fraction):
    return [
        -fraction * (fraction - 1.0) * (fraction - 2.0) / 6.0,
        (fraction + 1.0) * (fraction - 1.0) * (fraction - 2.0) / 2.0,
        -(fraction + 1.0) * fraction * (fraction - 2.0) / 2.0,
        (fraction + 1.0) * fraction * (fraction - 1.0) / 6.0,
    ]


def lon_adjoint(increments, lon_shift, lon_frac):
    row_count, fields, levels, points = increments.shape
    lon_weight = [w.astype(jnp.bfloat16) for w in lagrange(lon_frac)]
    source = jnp.arange(points, dtype=jnp.int32)[None, :, None]
    target = jnp.arange(points, dtype=jnp.int32)[None, None, :]
    width = math.gcd(row_count, 32)
    nothing = jnp.zeros((), jnp.bfloat16)

    def one_block(number):
        first = number * width
        shifts = lax.dynamic_slice_in_dim(lon_shift, first, width, 0)
        own_matrix = jnp.zeros((width, points, points), jnp.bfloat16)
        spill_matrix = jnp.zeros((width, points, points), jnp.bfloat16)
        for m in range(4):
            weight = lax.dynamic_slice_in_dim(lon_weight[m], first, width, 0)[:, :, None]
            landing = source + shifts[:, None, None] + m - 1
            own_matrix = own_matrix + jnp.where(target == landing, weight, nothing)
            wrapped = (target == landing - points) | (target == landing + points)
            spill_matrix = spill_matrix + jnp.where(wrapped, weight, nothing)
        values = lax.dynamic_slice_in_dim(increments, first, width, 0)
        own = jnp.einsum(
            "bflj,bjc->bflc", values, own_matrix, preferred_element_type=jnp.float32
        ).astype(jnp.bfloat16)
        spill = jnp.einsum(
            "bflj,bjc->bflc", values, spill_matrix, preferred_element_type=jnp.float32
        ).astype(jnp.bfloat16)
        return (own, spill)

    own, spill = lax.map(one_block, jnp.arange(row_count // width, dtype=jnp.int32))
    return (
        own.reshape(row_count, fields, levels, points),
        spill.reshape(row_count, fields, levels, points),
    )


def tile_terms(columns, own_rows, spill_rows):
    points = own_rows.shape[3]
    low_half = (jnp.arange(points, dtype=jnp.int32) < points // 2)[None, None, None, :]
    nothing = jnp.zeros((), jnp.bfloat16)
    spill_next = jnp.where(low_half, spill_rows, nothing)
    spill_prev = jnp.where(low_half, nothing, spill_rows)
    result = jnp.einsum("sq,sflc->lfqc", columns[0], own_rows, preferred_element_type=jnp.float32)
    result = result + jnp.einsum(
        "sq,sflc->lfqc", columns[1], spill_next, preferred_element_type=jnp.float32
    )
    return result + jnp.einsum(
        "sq,sflc->lfqc", columns[2], spill_prev, preferred_element_type=jnp.float32
    )


def local(increments, band, tile_index, lat_offset, lon_shift, lat_frac, lon_frac):
    row_count, fields, levels, points = increments.shape
    n_lat = lax.axis_size("lat")
    capacity = 3 * row_count // n_lat
    tile_rows = TILES_DEV * TL
    own, spill = lon_adjoint(increments, lon_shift, lon_frac)
    lat_weight = [w.astype(jnp.bfloat16) for w in lagrange(lat_frac)]
    tile_slots = jnp.arange(tile_rows, dtype=jnp.int32)[None, :]
    nothing = jnp.zeros((), jnp.bfloat16)

    def stencil_columns(tile_number):
        base_row = tile_number * TL + lat_offset
        table = jnp.zeros((row_count, tile_rows), jnp.bfloat16)
        for k in range(4):
            table = table + jnp.where(
                tile_slots == base_row[:, None] + k, lat_weight[k][:, None], nothing
            )
        return table

    here_columns = stencil_columns(tile_index)
    next_columns = stencil_columns((tile_index + 1) % TILES_DEV)
    prev_columns = stencil_columns((tile_index + TILES_DEV - 1) % TILES_DEV)
    destination = band[:, 0]
    one_hot = (destination[:, None] == jnp.arange(n_lat, dtype=jnp.int32)[None, :]).astype(
        jnp.int32
    )
    position = jnp.sum(jnp.cumsum(one_hot, axis=0) * one_hot, axis=1) - 1
    slot_index = destination * capacity + position

    def to_slots(values):
        empty = jnp.zeros((n_lat * capacity,) + values.shape[1:], jnp.bfloat16)
        placed = empty.at[slot_index].set(values)
        return placed.reshape((n_lat, capacity) + values.shape[1:])

    send_own = to_slots(own)
    send_spill = to_slots(spill)
    send_here = to_slots(here_columns)
    send_next = to_slots(next_columns)
    send_prev = to_slots(prev_columns)
    got = (
        lax.all_to_all(send_own, "lat", split_axis=0, concat_axis=0, tiled=True),
        lax.all_to_all(send_spill, "lat", split_axis=0, concat_axis=0, tiled=True),
        lax.all_to_all(send_here, "lat", split_axis=0, concat_axis=0, tiled=True),
        lax.all_to_all(send_next, "lat", split_axis=0, concat_axis=0, tiled=True),
        lax.all_to_all(send_prev, "lat", split_axis=0, concat_axis=0, tiled=True),
    )
    flat_own = got[0].reshape(-1, fields, levels, points)
    flat_spill = got[1].reshape(-1, fields, levels, points)
    flat_columns = (
        got[2].reshape(-1, tile_rows),
        got[3].reshape(-1, tile_rows),
        got[4].reshape(-1, tile_rows),
    )
    return summed_on_arrival(tile_terms(flat_columns, flat_own, flat_spill), "grp", 0)


def solution(mesh):
    in_specs = (
        P(("lat", "grp"), None, None, None),
        P(("lat", "grp"), None),
        P(("lat", "grp")),
        P(("lat", "grp")),
        P(("lat", "grp")),
        P(("lat", "grp")),
        P(("lat", "grp"), None),
    )
    out_specs = P("grp", None, "lat", None)
    return jax.shard_map(local, mesh=mesh, in_specs=in_specs, out_specs=out_specs, check_vma=False)
```

profile of v0, /device:TPU:1, one launch (start us, length us, event | category | flops | bytes accessed | tf_op | source)
XLA Modules:
  0.0 389.2 jit_solution(10969625187045587971)
XLA Ops:
  2.2 0.8 select_reduce_fusion
  3.7 0.9 scatter_custom_fusion.4
  5.2 15.6 %all-to-all-start.4 = ((bf16[64,3,128]{2,1,0:T(4,128)(2,1)}), bf16[64,3,128]{2,1,0:T(4,128)(2,1)S(1)}, u32[]{:S(2)}, u32[]{:S(2)}) async-start(bf16[64,3,128]{2,1,0:T(4,128)(2,1)} %reshape.471), calls=%async_computation.4 | async-start | bytes 131072 | tf_op jit(solution)/shard_map/all_to_all | solution.py:127
  20.9 0.8 fusion.95
  21.7 0.9 scatter_custom_fusion.3
  23.2 9.6 %all-to-all-done.4 = bf16[64,3,128]{2,1,0:T(4,128)(2,1)S(1)} async-done(((bf16[64,3,128]{2,1,0:T(4,128)(2,1)}), bf16[64,3,128]{2,1,0:T(4,128)(2,1)S(1)}, u32[]{:S(2)}, u32[]{:S(2)}) %all-to-all-start.4) | async-done | bytes 49184 | tf_op jit(solution)/shard_map/all_to_all | solution.py:127
  32.8 4.5 %all-to-all-start.3 = ((bf16[64,3,128]{2,1,0:T(4,128)(2,1)}), bf16[64,3,128]{2,1,0:T(4,128)(2,1)S(1)}, u32[]{:S(2)}, u32[]{:S(2)}) async-start(bf16[64,3,128]{2,1,0:T(4,128)(2,1)} %reshape.470), calls=%async_computation.3 | async-start | bytes 131072 | tf_op jit(solution)/shard_map/all_to_all | solution.py:126
  37.4 0.9 scatter_custom_fusion.1
  38.9 10.5 %all-to-all-done.3 = bf16[64,3,128]{2,1,0:T(4,128)(2,1)S(1)} async-done(((bf16[64,3,128]{2,1,0:T(4,128)(2,1)}), bf16[64,3,128]{2,1,0:T(4,128)(2,1)S(1)}, u32[]{:S(2)}, u32[]{:S(2)}) %all-to-all-start.3) | async-done | bytes 49184 | tf_op jit(solution)/shard_map/all_to_all | solution.py:126
  49.4 4.5 %all-to-all-start.1 = ((bf16[64,3,128]{2,1,0:T(4,128)(2,1)}), bf16[64,3,128]{2,1,0:T(4,128)(2,1)S(1)}, u32[]{:S(2)}, u32[]{:S(2)}) async-start(bf16[64,3,128]{2,1,0:T(4,128)(2,1)} %reshape.467), calls=%async_computation.1 | async-start | bytes 131072 | tf_op jit(solution)/shard_map/all_to_all | solution.py:125
  53.9 44.4 %while.19 = (s32[]{:T(128)}, bf16[2,32,4,16,128]{4,3,2,1,0:T(8,128)(2,1)S(1)}, bf16[2,32,4,16,128]{4,3,2,1,0:T(8,128)(2,1)S(1)}, s32[2]{0:T(128)S(1)}, bf16[64,4...) while((s32[]{:T(128)}, ...), condition=%wide.region_3.4_spmd.clone.clone, body=%wide.region_2.3_spmd.clone.clone.sunk | while | flops 155762688 | bytes 6816383 | solution.py:61
  55.2 0.7 dynamic_slice.104
  56.1 7.2 %fusion.184 = bf16[2,32,4,16,128]{4,3,2,1,0:T(8,128)(2,1)S(1)} fusion(bf16[2,32,4,16,128]{4,3,2,1,0:T(8,128)(2,1)S(1)} %get-tuple-element.552, s32[]{:T(128)S(6)} %copy.67, s32[32,128]{1,0:T(8,128)S(1)} %get-tuple-element.521, s32[32,128]{1,0:T(8,128)S(1)} %get-tuple-element.522, s32[32,128]{1,0:T(8,128)S(1)} %get-tuple-element.523, ...), kind=kOutput, calls=%fused_computation.34.clone.1 | convolution fusion | flops 75759616 | bytes 1146888 | tf_op jit(solution)/shard_map/while/body/eval_jaxpr/bflj,bjc->bflc/dot_general | solution.py:53
  63.3 12.8 %fusion.185 = bf16[2,32,4,16,128]{4,3,2,1,0:T(8,128)(2,1)S(1)} fusion(bf16[2,32,4,16,128]{4,3,2,1,0:T(8,128)(2,1)S(1)} %get-tuple-element.553, s32[]{:T(128)S(6)} %copy.67, s32[32,128]{1,0:T(8,128)S(1)} %get-tuple-element.529, s32[32,128]{1,0:T(8,128)S(1)} %get-tuple-element.530, s32[32,128]{1,0:T(8,128)S(1)} %get-tuple-element.531, ...), kind=kOutput, calls=%fused_computation.36.clone.1 | convolution fusion | flops 79953920 | bytes 1212424 | tf_op jit(solution)/shard_map/while/body/eval_jaxpr/bflj,bjc->bflc/dot_general | solution.py:56
  77.4 0.7 dynamic_slice.104
  78.2 7.2 %fusion.184 = bf16[2,32,4,16,128]{4,3,2,1,0:T(8,128)(2,1)S(1)} fusion(bf16[2,32,4,16,128]{4,3,2,1,0:T(8,128)(2,1)S(1)} %get-tuple-element.552, s32[]{:T(128)S(6)} %copy.67, s32[32,128]{1,0:T(8,128)S(1)} %get-tuple-element.521, s32[32,128]{1,0:T(8,128)S(1)} %get-tuple-element.522, s32[32,128]{1,0:T(8,128)S(1)} %get-tuple-element.523, ...), kind=kOutput, calls=%fused_computation.34.clone.1 | convolution fusion | flops 75759616 | bytes 1146888 | tf_op jit(solution)/shard_map/while/body/eval_jaxpr/bflj,bjc->bflc/dot_general | solution.py:53
  85.5 12.8 %fusion.185 = bf16[2,32,4,16,128]{4,3,2,1,0:T(8,128)(2,1)S(1)} fusion(bf16[2,32,4,16,128]{4,3,2,1,0:T(8,128)(2,1)S(1)} %get-tuple-element.553, s32[]{:T(128)S(6)} %copy.67, s32[32,128]{1,0:T(8,128)S(1)} %get-tuple-element.529, s32[32,128]{1,0:T(8,128)S(1)} %get-tuple-element.530, s32[32,128]{1,0:T(8,128)S(1)} %get-tuple-element.531, ...), kind=kOutput, calls=%fused_computation.36.clone.1 | convolution fusion | flops 79953920 | bytes 1212424 | tf_op jit(solution)/shard_map/while/body/eval_jaxpr/bflj,bjc->bflc/dot_general | solution.py:56
  98.3 2.5 broadcast.675.clone
  100.8 8.1 %scatter_fusion.1 = bf16[192,4,16,128]{3,2,1,0:T(8,128)(2,1)} fusion(bf16[192,4,16,128]{3,2,1,0:T(8,128)(2,1)} %broadcast.675.clone, s32[64]{0:T(128)S(1)} %fusion.169, bf16[64,4,16,128]{3,2,1,0:T(8,128)(2,1)S(1)} %bitcast.64), kind=kCustom, calls=%fused_computation.2 | custom fusion | bytes 3145984 | tf_op jit(solution)/shard_map/scatter | solution.py:114
  108.9 13.0 %all-to-all-start.2 = ((bf16[64,3,4,16,128]{4,3,2,1,0:T(8,128)(2,1)}), bf16[64,3,4,16,128]{4,3,2,1,0:T(8,128)(2,1)}, u32[]{:S(2)}, u32[]{:S(2)}) async-start(bf16[64,3,4,16,128]{4,3,2,1,0:T(8,128)(2,1)} %bitcast.9), calls=%async_computation.2 | async-start | bytes 6291456 | tf_op jit(solution)/shard_map/all_to_all | solution.py:124
  122.0 0.8 broadcast.675.clone.1
  122.7 6.2 %scatter_fusion = bf16[192,4,16,128]{3,2,1,0:T(8,128)(2,1)S(1)} fusion(bf16[192,4,16,128]{3,2,1,0:T(8,128)(2,1)S(1)} %broadcast.675.clone.1, s32[64]{0:T(128)S(1)} %fusion.169, bf16[64,4,16,128]{3,2,1,0:T(8,128)(2,1)} %bitcast.65), kind=kCustom, calls=%fused_computation | custom fusion | bytes 3145984 | tf_op jit(solution)/shard_map/scatter | solution.py:114
  129.0 70.6 %all-to-all-done.2 = bf16[64,3,4,16,128]{4,3,2,1,0:T(8,128)(2,1)} async-done(((bf16[64,3,4,16,128]{4,3,2,1,0:T(8,128)(2,1)}), bf16[64,3,4,16,128]{4,3,2,1,0:T(8,128)(2,1)}, u32[]{:S(2)}, u32[]{:S(2)}) %all-to-all-start.2) | async-done | bytes 3145760 | tf_op jit(solution)/shard_map/all_to_all | solution.py:124
  199.6 4.5 %all-to-all-start = ((bf16[64,3,4,16,128]{4,3,2,1,0:T(8,128)(2,1)}), bf16[64,3,4,16,128]{4,3,2,1,0:T(8,128)(2,1)S(1)}, u32[]{:S(2)}, u32[]{:S(2)}) async-start(bf16[64,3,4,16,128]{4,3,2,1,0:T(8,128)(2,1)} %bitcast.63), calls=%async_computation | async-start | bytes 6291456 | tf_op jit(solution)/shard_map/all_to_all | solution.py:123
  204.1 2.3 broadcast_select_fusion.1
  206.4 6.1 %fusion.77 = f32[4,16,128,128,1]{3,2,4,1,0:T(8,128)} fusion(bf16[64,3,4,16,128]{4,3,2,1,0:T(8,128)(2,1)S(1)} %get-tuple-element.424, bf16[64,3,128,1,1]{2,1,0,4,3:T(4,128)(2,1)S(1)} %bitcast.67), kind=kOutput, calls=%fused_computation.93 | convolution fusion | flops 402653184 | bytes 7389184 | tf_op jit(solution)/shard_map/sq,sflc->lfqc/dot_general | solution.py:75
  212.5 6.0 %fusion.75 = f32[4,16,128,128,1]{3,2,4,1,0:T(8,128)} fusion(bf16[64,3,4,16,128]{4,3,2,1,0:T(8,128)(2,1)S(1)} %get-tuple-element.425, bf16[64,3,128,1,1]{2,1,0,4,3:T(4,128)(2,1)S(1)} %bitcast.66), kind=kOutput, calls=%fused_computation.91 | convolution fusion | flops 402653184 | bytes 7389184 | tf_op jit(solution)/shard_map/sq,sflc->lfqc/dot_general | solution.py:78
  218.5 29.1 %all-to-all-done = bf16[64,3,4,16,128]{4,3,2,1,0:T(8,128)(2,1)S(1)} async-done(((bf16[64,3,4,16,128]{4,3,2,1,0:T(8,128)(2,1)}), bf16[64,3,4,16,128]{4,3,2,1,0:T(8,128)(2,1)S(1)}, u32[]{:S(2)}, u32[]{:S(2)}) %all-to-all-start) | async-done | bytes 3145760 | tf_op jit(solution)/shard_map/all_to_all | solution.py:123
  247.6 7.9 %bitcast_add_fusion = f32[4,16,128,128]{3,2,1,0:T(8,128)S(1)} fusion(f32[4,16,128,128,1]{3,2,4,1,0:T(8,128)} %fusion.75, f32[4,16,128,128,1]{3,2,4,1,0:T(8,128)} %fusion.77, bf16[64,3,4,16,128]{4,3,2,1,0:T(8,128)(2,1)S(1)} %all-to-all-done, bf16[64,3,128,1,1]{2,1,0,4,3:T(4,128)(2,1)S(1)} %bitcast.68), kind=kOutput, calls=%fused_computation.89 | convolution fusion | flops 404750336 | bytes 15777792 | tf_op jit(solution)/shard_map/sq,sflc->lfqc/dot_general | solution.py:74
  256.0 129.4 %all_to_all.30 = f32[4,4,4,128,128]{3,4,1,2,0:T(8,128)} all-to-all(f32[4,4,4,128,128]{3,4,1,2,0:T(8,128)S(1)} %copy.30), channel_id=1, replica_groups=mesh['lat'=64,'grp'=4] {'grp'}, dimensions={0} | all-to-all | bytes 8388608 | tf_op jit(solution)/shard_map/all_to_all | solution.py:20
  385.3 2.6 reduce_sum.19
  387.9 1.3 copy.32
  (33 shorter events, 6.8 us)
Async XLA Ops:
  5.2 27.6 %all-to-all-start.4 = ((bf16[64,3,128]{2,1,0:T(4,128)(2,1)}), bf16[64,3,128]{2,1,0:T(4,128)(2,1)S(1)}, u32[]{:S(2)}, u32[]{:S(2)}) async-start(bf16[64,3,128]{2,1,0:T(4,128)(2,1)} %reshape.471), calls=%async_computation.4 | async-start | bytes 131072 | tf_op jit(solution)/shard_map/all_to_all | solution.py:127
  32.8 16.6 %all-to-all-start.3 = ((bf16[64,3,128]{2,1,0:T(4,128)(2,1)}), bf16[64,3,128]{2,1,0:T(4,128)(2,1)S(1)}, u32[]{:S(2)}, u32[]{:S(2)}) async-start(bf16[64,3,128]{2,1,0:T(4,128)(2,1)} %reshape.470), calls=%async_computation.3 | async-start | bytes 131072 | tf_op jit(solution)/shard_map/all_to_all | solution.py:126
  49.4 59.5 %all-to-all-start.1 = ((bf16[64,3,128]{2,1,0:T(4,128)(2,1)}), bf16[64,3,128]{2,1,0:T(4,128)(2,1)S(1)}, u32[]{:S(2)}, u32[]{:S(2)}) async-start(bf16[64,3,128]{2,1,0:T(4,128)(2,1)} %reshape.467), calls=%async_computation.1 | async-start | bytes 131072 | tf_op jit(solution)/shard_map/all_to_all | solution.py:125
  56.0 7.3 %copy-start.2 = (bf16[64,4,16,128]{3,2,1,0:T(8,128)(2,1)S(1)}, bf16[64,4,16,128]{3,2,1,0:T(8,128)(2,1)}, u32[]{:S(2)}) copy-start(bf16[64,4,16,128]{3,2,1,0:T(8,128)(2,1)} %get-tuple-element.569) | copy-start | bytes 3145732 | tf_op jit(solution)/shard_map/while
  78.2 7.3 %copy-start.2 = (bf16[64,4,16,128]{3,2,1,0:T(8,128)(2,1)S(1)}, bf16[64,4,16,128]{3,2,1,0:T(8,128)(2,1)}, u32[]{:S(2)}) copy-start(bf16[64,4,16,128]{3,2,1,0:T(8,128)(2,1)} %get-tuple-element.569) | copy-start | bytes 3145732 | tf_op jit(solution)/shard_map/while
  98.3 10.6 %copy-start.1 = (bf16[2,32,4,16,128]{4,3,2,1,0:T(8,128)(2,1)}, bf16[2,32,4,16,128]{4,3,2,1,0:T(8,128)(2,1)S(1)}, u32[]{:S(2)}) copy-start(bf16[2,32,4,16,128]{4,3,2,1,0:T(8,128)(2,1)S(1)} %get-tuple-element.319) | copy-start | bytes 3145732
  108.9 90.7 %all-to-all-start.2 = ((bf16[64,3,4,16,128]{4,3,2,1,0:T(8,128)(2,1)}), bf16[64,3,4,16,128]{4,3,2,1,0:T(8,128)(2,1)}, u32[]{:S(2)}, u32[]{:S(2)}) async-start(bf16[64,3,4,16,128]{4,3,2,1,0:T(8,128)(2,1)} %bitcast.9), calls=%async_computation.2 | async-start | bytes 6291456 | tf_op jit(solution)/shard_map/all_to_all | solution.py:124
  129.0 70.6 %copy-start = (bf16[192,4,16,128]{3,2,1,0:T(8,128)(2,1)}, bf16[192,4,16,128]{3,2,1,0:T(8,128)(2,1)S(1)}, u32[]{:S(2)}) copy-start(bf16[192,4,16,128]{3,2,1,0:T(8,128)(2,1)S(1)} %scatter_fusion) | copy-start | bytes 9437188
  199.6 48.0 %all-to-all-start = ((bf16[64,3,4,16,128]{4,3,2,1,0:T(8,128)(2,1)}), bf16[64,3,4,16,128]{4,3,2,1,0:T(8,128)(2,1)S(1)}, u32[]{:S(2)}, u32[]{:S(2)}) async-start(bf16[64,3,4,16,128]{4,3,2,1,0:T(8,128)(2,1)} %bitcast.63), calls=%async_computation | async-start | bytes 6291456 | tf_op jit(solution)/shard_map/all_to_all | solution.py:123
where the time goes:
time: 391 us; the launch traced here: 389 us
  blocking collectives  129 us (33%)
  waiting for transfers between devices  120 us (31%)
  matrix products  60 us (15%)
  starting transfers between devices  42.1 us (11%)
  local copies, waits for them, and re-layouts  24.1 us (6%)
  other arithmetic  12.2 us (3%)
    all_to_all x1, blocking collectives, summed_on_arrival(): pieces = lax.all_to_all(cut_along(array, dim, size), axis, 0, 0, tiled=True)  129 us
    all_to_all x1, waiting for transfers between devices, local(): lax.all_to_all(send_spill, 'lat', split_axis=0, concat_axis=0, tiled=True)  70.6 us
    all_to_all x1, waiting for transfers between devices, local(): lax.all_to_all(send_own, 'lat', split_axis=0, concat_axis=0, tiled=True)  29.1 us
    dot_general x2, matrix products, one_block(): jnp.einsum('bflj,bjc->bflc', values, spill_matrix, preferred_element_type...  25.6 us
    all_to_all x1, starting transfers between devices, local(): lax.all_to_all(send_prev, 'lat', split_axis=0, concat_axis=0, tiled=True)  15.6 us
    dot_general x2, matrix products, one_block(): jnp.einsum('bflj,bjc->bflc', values, own_matrix, preferred_element_type=j...  14.5 us
    scatter x2, local copies, waits for them, and re-layouts, to_slots(): placed = empty.at[slot_index].set(values)  14.4 us
    all_to_all x1, starting transfers between devices, local(): lax.all_to_all(send_spill, 'lat', split_axis=0, concat_axis=0, tiled=True)  13 us
  transfers between devices with their start and end apart: 5, of which 4 were waited for; matrix products, arithmetic and copies ran while one was open for 20% of the time, Pallas kernels for 0%

commit v1 on v0

v1 whole, which is shorter than its diff:
```python
import jax
import jax.numpy as jnp
from jax import lax
from jax.experimental import pallas as pl
from jax.experimental.pallas import tpu as pltpu
from jax.sharding import PartitionSpec as P

TL = 16
CAP = 3
SLOT_ROWS = 16
OWN_ROWS = CAP * SLOT_ROWS
PEER_ROWS = OWN_ROWS + 8
META_ROW = 6


def lagrange(fraction):
    return [
        -fraction * (fraction - 1.0) * (fraction - 2.0) / 6.0,
        (fraction + 1.0) * (fraction - 1.0) * (fraction - 2.0) / 2.0,
        -(fraction + 1.0) * fraction * (fraction - 2.0) / 2.0,
        (fraction + 1.0) * fraction * (fraction - 1.0) / 6.0,
    ]


def rounded(x):
    return x.astype(jnp.bfloat16).astype(jnp.float32)


def source_kernel(
    band, tile_index, lat_offset, lon_shift, lat_frac, inc, lon_frac, out, weights, extra, count
):
    rows = inc.shape[0]
    bands = out.shape[0] // 4
    lane = lax.broadcasted_iota(jnp.int32, (8, 128), 1)
    sub = lax.broadcasted_iota(jnp.int32, (8, 128), 0)
    zero = jnp.zeros((8, 128), jnp.float32)

    for m, w in enumerate(lagrange(lon_frac[...])):
        weights[m] = rounded(w)

    def clear(i, _):
        out[pl.ds(i * 4, 4)] = jnp.zeros((4,) + out.shape[1:], jnp.bfloat16)
        extra[pl.ds(i * 4, 4)] = jnp.zeros((4, 8, 128), jnp.float32)
        count[i] = 0
        return 0

    lax.fori_loop(0, bands, clear, 0)

    def one_row(r, _):
        b = band[r]
        slot = count[b]
        count[b] = slot + 1
        shift = lon_shift[r]
        x = inc[r].astype(jnp.float32)
        half = [[x[f, 8 * h : 8 * h + 8] for h in range(2)] for f in range(4)]
        pieces = []
        for g in range(4):
            h, odd = g // 2, g % 2
            for f in (0, 2):
                first, second = half[f][h], half[f + 1][h]
                if odd:
                    first = pltpu.roll(first, 4, 0)
                else:
                    second = pltpu.roll(second, 4, 0)
                pieces.append(jnp.where(sub < 4, first, second))
        own = [zero] * 8
        spill = [zero] * 8
        for m in range(4):
            move = (shift + (m - 1 + 128)) & 127
            w = jnp.broadcast_to(weights[m, pl.ds(r, 1), :], (8, 128))
            w = pltpu.roll(w, move, 1)
            raw = lane - shift - (m - 1)
            inside = (raw >= 0) & (raw < 128)
            own_w = jnp.where(inside, w, 0.0)
            spill_w = jnp.where(inside, 0.0, w)
            for i in range(8):
                moved = pltpu.roll(pieces[i], move, 1)
                own[i] = own[i] + own_w * moved
                spill[i] = spill[i] + spill_w * moved
        spot = lane - 8 * slot
        lat = lagrange(jnp.full((8, 128), lat_frac[r], jnp.float32))
        first_row = (tile_index[r] * TL + lat_offset[r]).astype(jnp.float32)
        meta = jnp.where(spot == 0, first_row, jnp.where(spot == 1, shift.astype(jnp.float32), 0.0))
        for k in range(4):
            meta = jnp.where(spot == 2 + k, lat[k], meta)
        base = jnp.where(sub == META_ROW, meta, 0.0)
        at = pl.multiple_of(slot * SLOT_ROWS, SLOT_ROWS)
        for g in range(4):
            block = jnp.concatenate([own[2 * g], own[2 * g + 1]], axis=0)
            out[b * 4 + g, pl.ds(at, SLOT_ROWS), :] = block.astype(jnp.bfloat16)
            tile = base
            for h in range(2):
                s = spill[2 * g + h]
                folded = jnp.where(lane < 16, s + pltpu.roll(s, 16, 1), 0.0)
                spread = pltpu.roll(folded, 0, 1, stride=16, stride_axis=0)
                line = jnp.sum(spread, axis=0, keepdims=True)
                tile = jnp.where(sub == 2 * slot + h, line, tile)
            extra[b * 4 + g] = extra[b * 4 + g] + tile
        return 0

    lax.fori_loop(0, rows, one_row, 0)

    def finish(i, _):
        out[pl.ds(i * 4, 4), OWN_ROWS:PEER_ROWS, :] = extra[pl.ds(i * 4, 4)].astype(jnp.bfloat16)
        return 0

    lax.fori_loop(0, bands, finish, 0)


def tile_kernel(got, out, wide, extra):
    peers = got.shape[0]

    def widen(p, _):
        wide[pl.ds(pl.multiple_of(p * OWN_ROWS, 8), OWN_ROWS), :] = got[p, 0:OWN_ROWS, :].astype(jnp.float32)
        extra[pl.ds(pl.multiple_of(p * 8, 8), 8), :] = got[p, OWN_ROWS:PEER_ROWS, :].astype(jnp.float32)
        return 0

    lax.fori_loop(0, peers, widen, 0, unroll=4)

    meta = extra[pl.ds(META_ROW, peers, stride=8), :]
    row_id = lax.broadcasted_iota(jnp.int32, (peers, 128), 1).astype(jnp.float32)
    place = lax.broadcasted_iota(jnp.int32, (peers, 128), 1) % 16
    stencil, spill_next, spill_prev = [], [], []
    for j in range(CAP):
        c = 8 * j
        table = jnp.zeros((peers, 128), jnp.float32)
        first_row = meta[:, c : c + 1]
        for k in range(4):
            table = table + jnp.where(row_id == first_row + float(k), meta[:, c + 2 + k : c + 3 + k], 0.0)
        stencil.append(table.T.astype(jnp.bfloat16))
        shift = meta[:, c + 1 : c + 2]
        forward = (shift > 0.5) | ((shift > -1.5) & (place < 8))
        lines = [extra[pl.ds(2 * j + h, peers, stride=8), :] for h in range(2)]
        spill_next.append(jnp.concatenate([jnp.where(forward, s, 0.0) for s in lines], axis=1).astype(jnp.bfloat16))
        spill_prev.append(jnp.concatenate([jnp.where(forward, 0.0, s) for s in lines], axis=1).astype(jnp.bfloat16))
    columns = jnp.concatenate(stencil, axis=1)

    def product(values):
        return jnp.dot(columns, jnp.concatenate(values, axis=0), preferred_element_type=jnp.float32)

    onward = product(spill_next)
    onward = jnp.concatenate([onward[128 - TL :], onward[: 128 - TL]], axis=0)
    back = product(spill_prev)
    back = jnp.concatenate([back[TL:], back[:TL]], axis=0)
    lane = lax.broadcasted_iota(jnp.int32, (128, 128), 1)
    for pair in range(8):
        values = []
        for j in range(CAP):
            cols = [
                wide[pl.ds(j * SLOT_ROWS + 2 * pair + e, peers, stride=OWN_ROWS), :].astype(jnp.bfloat16)
                for e in range(2)
            ]
            values.append(jnp.concatenate(cols, axis=1))
        total = product(values)
        for e in range(2):
            fl = 2 * pair + e
            h, i = fl // 8, fl % 8
            ahead = pltpu.roll(onward[:, 128 * h : 128 * h + 128], (128 - 16 * i) % 128, 1)
            behind = pltpu.roll(back[:, 128 * h : 128 * h + 128], (112 - 16 * i) % 128, 1)
            edges = jnp.where(lane < 16, ahead, jnp.where(lane >= 112, behind, 0.0))
            out[fl % 4, fl // 4] = total[:, 128 * e : 128 * e + 128] + edges


def local(increments, band, tile_index, lat_offset, lon_shift, lat_frac, lon_frac):
    rows = increments.shape[0]
    n_lat = lax.axis_size("lat")
    peers = 4 * n_lat
    smem = pl.BlockSpec(memory_space=pltpu.SMEM)
    vmem = pl.BlockSpec(memory_space=pltpu.VMEM)
    send = pl.pallas_call(
        source_kernel,
        out_shape=jax.ShapeDtypeStruct((peers, PEER_ROWS, 128), jnp.bfloat16),
        in_specs=[smem] * 5 + [vmem] * 2,
        out_specs=vmem,
        scratch_shapes=[
            pltpu.VMEM((4, rows, 128), jnp.float32),
            pltpu.VMEM((peers, 8, 128), jnp.float32),
            pltpu.SMEM((n_lat,), jnp.int32),
        ],
        compiler_params=pltpu.CompilerParams(vmem_limit_bytes=24 << 20),
        name="lon_slots",
    )(band.reshape(rows), tile_index, lat_offset, lon_shift, lat_frac, increments, lon_frac)
    got = lax.all_to_all(send, ("lat", "grp"), 0, 0, tiled=True)
    return pl.pallas_call(
        tile_kernel,
        out_shape=jax.ShapeDtypeStruct((4, 4, 128, 128), jnp.float32),
        in_specs=[vmem],
        out_specs=vmem,
        scratch_shapes=[
            pltpu.VMEM((peers * OWN_ROWS, 128), jnp.float32),
            pltpu.VMEM((peers * 8, 128), jnp.float32),
        ],
        compiler_params=pltpu.CompilerParams(vmem_limit_bytes=40 << 20),
        name="tile_sums",
    )(got)


def solution(mesh):
    in_specs = (
        P(("lat", "grp"), None, None, None),
        P(("lat", "grp"), None),
        P(("lat", "grp")),
        P(("lat", "grp")),
        P(("lat", "grp")),
        P(("lat", "grp")),
        P(("lat", "grp"), None),
    )
    out_specs = P("grp", None, "lat", None)
    return jax.shard_map(local, mesh=mesh, in_specs=in_specs, out_specs=out_specs, check_vma=False)
```

time: 391 us -> 131 us (0.34)
  waiting for transfers between devices: 120 us -> 0 us
  matrix products: 60 us -> 0 us
  starting transfers between devices: 42.1 us -> 0 us
  blocking collectives: 129 us -> 103 us
  Pallas kernels: 0 us -> 22.5 us
  local copies, waits for them, and re-layouts: 24.1 us -> 5.26 us
  other arithmetic: 12.2 us -> 0 us
    all_to_all x5 -> x0, waiting for transfers between devices: 120 us -> none  [the longest x1 70.6 us: local(): lax.all_to_all(send_spill, 'lat', split_axis=0, concat_axis=0, tiled=True)]
    dot_general x7 -> x0, matrix products: 60 us -> none  [the longest x2 25.6 us: one_block(): jnp.einsum('bflj,bjc->bflc', values, spill_matrix, preferred_element_type...]
    all_to_all x5 -> x0, starting transfers between devices: 42.1 us -> none  [the longest x1 15.6 us: local(): lax.all_to_all(send_prev, 'lat', split_axis=0, concat_axis=0, tiled=True)]
    all_to_all x1, blocking collectives: 129 us -> 103 us  [local(): got = lax.all_to_all(send, ('lat', 'grp'), 0, 0, tiled=True)]
    pallas_call x0 -> x2, Pallas kernels: none -> 22.5 us  [the longest x1 17.3 us: local(): pl.pallas_call(source_kernel, out_shape=jax.ShapeDtypeStruct((peers, PEER...]
    scatter x2 -> x0, local copies, waits for them, and re-layouts: 14.4 us -> none  [to_slots(): placed = empty.at[slot_index].set(values)]
    unnamed x4 -> x14, local copies, waits for them, and re-layouts: 0.01 us -> 5.26 us
  transfers between devices with their start and end apart: 5 -> 0, of which waited for: 4 -> 0; matrix products, arithmetic and copies ran while one was open for 20% -> 0% of each run, Pallas kernels for 0% -> 0%
where the time goes in v1:
time: 131 us
  blocking collectives  103 us (79%)
  Pallas kernels  22.5 us (17%)
  local copies, waits for them, and re-layouts  5.26 us (4%)
    all_to_all x1, blocking collectives, local(): got = lax.all_to_all(send, ('lat', 'grp'), 0, 0, tiled=True)  103 us
    pallas_call x1, Pallas kernels, local(): pl.pallas_call(source_kernel, out_shape=jax.ShapeDtypeStruct((peers, PEER...  17.3 us
    pallas_call x1, Pallas kernels, local(): pl.pallas_call(tile_kernel, out_shape=jax.ShapeDtypeStruct((4, 4, 128, 12...  5.26 us
    unnamed x14, local copies, waits for them, and re-layouts  5.26 us

profile of v1, /device:TPU:1, one launch (start us, length us, event | category | flops | bytes accessed | tf_op | source)
XLA Modules:
  0.0 131.2 jit_solution(14961857762847036092)
XLA Ops:
  0.0 0.0 copy-start
  0.0 1.2 copy-done
  1.2 0.0 copy-start.1
  1.2 0.8 copy-done.1
  2.0 0.0 copy-start.2
  2.0 0.7 copy-done.2
  2.6 0.0 copy-start.3
  2.6 0.7 copy-done.3
  3.3 0.0 copy-start.4
  3.3 0.7 copy-done.4
  4.0 0.0 copy-start.5
  4.0 0.7 copy-done.5
  4.6 0.0 copy-start.6
  4.6 0.7 copy-done.6
  5.3 17.3 %lon_slots.1 = bf16[256,56,128]{2,1,0:T(8,128)(2,1)S(1)} custom-call(s32[64]{0:T(128)S(1)} %bitcast.1, s32[64]{0:T(128)S(1)} %copy-done.3, s32[64]{0:T(128)S(1)} %copy-done.4, s32[64]{0:T(128)S(1)} %copy-done.5, f32[64]{0:T(128)S(1)} %copy-done.6, bf16[64,4,16,128]{3,2,1,0:T(8,128)(2,1)S(1)} %copy-done, f32[64,128]{1,0:T(8,128)S(1)} %copy-done.1), custom_call_target="tpu_custom_call" | custom-call | tf_op jit(solution)/shard_map/lon_slots/pallas_call | solution.py:170
  22.5 103.4 %all_to_all.5.got = bf16[256,56,128]{2,1,0:T(8,128)(2,1)S(1)} all-to-all(bf16[256,56,128]{2,1,0:T(8,128)(2,1)S(1)} %lon_slots.1), channel_id=1, replica_groups=mesh['lat'=64,'grp'=4] {'lat','grp'}, dimensions={0} | all-to-all | bytes 7340032 | tf_op jit(solution)/shard_map/all_to_all | solution.py:183
  125.9 5.3 %tile_sums.1 = f32[4,4,128,128]{3,2,1,0:T(8,128)} custom-call(bf16[256,56,128]{2,1,0:T(8,128)(2,1)S(1)} %all_to_all.5.got), custom_call_target="tpu_custom_call" | custom-call | tf_op jit(solution)/shard_map/tile_sums/pallas_call | solution.py:184
Async XLA Ops:
  0.0 1.2 copy-start
  1.2 0.8 copy-start.1
  2.0 0.7 copy-start.2
  2.6 0.7 copy-start.3
  3.3 0.7 copy-start.4
  4.0 0.7 copy-start.5
  4.6 0.7 copy-start.6

commit v2 on v1

v2 whole, which is shorter than its diff:
```python
import jax
import jax.numpy as jnp
from jax import lax
from jax.experimental import pallas as pl
from jax.experimental.pallas import tpu as pltpu
from jax.sharding import PartitionSpec as P

TL = 16
CAP = 3
SLOT_ROWS = 16
OWN_ROWS = CAP * SLOT_ROWS
PEER_ROWS = OWN_ROWS + CAP + 1
EDGE = 10
WHOLE = 12
META = EDGE * WHOLE


def lagrange(fraction):
    return [
        -fraction * (fraction - 1.0) * (fraction - 2.0) / 6.0,
        (fraction + 1.0) * (fraction - 1.0) * (fraction - 2.0) / 2.0,
        -(fraction + 1.0) * fraction * (fraction - 2.0) / 2.0,
        (fraction + 1.0) * fraction * (fraction - 1.0) / 6.0,
    ]


def rounded(x):
    return x.astype(jnp.bfloat16).astype(jnp.float32)


def source_kernel(
    band_hbm, tile_hbm, offset_hbm, shift_hbm, lat_hbm, inc_hbm, lon_hbm, out,
    band, tile_index, lat_offset, lon_shift, lat_frac, count, first, slot_of,
    inc, lon_frac, weights, stage, edges, meta_lines, lines, sems,
):
    rows = inc.shape[0]
    bands = count.shape[0]
    pairs = (
        (band_hbm, band), (tile_hbm, tile_index), (offset_hbm, lat_offset), (shift_hbm, lon_shift),
        (lat_hbm, lat_frac), (lon_hbm, lon_frac), (inc_hbm, inc),
    )
    copies = [pltpu.make_async_copy(src, dst, sems.at[i]) for i, (src, dst) in enumerate(pairs)]
    for copy in copies:
        copy.start()

    lane = lax.broadcasted_iota(jnp.int32, (8, 128), 1)
    sub = lax.broadcasted_iota(jnp.int32, (8, 128), 0)
    zero = jnp.zeros((8, 128), jnp.float32)
    part = stage.shape[0] // bands

    def clear(i, _):
        stage[pl.ds(pl.multiple_of(i * part, 8), part), :] = jnp.zeros((part, 128), jnp.float32)
        count[i] = 0
        return 0

    lax.fori_loop(0, bands, clear, 0)
    for copy in copies:
        copy.wait()

    for m, w in enumerate(lagrange(lon_frac[...])):
        weights[m] = rounded(w)

    def one_row(r, _):
        b = band[r]
        slot = count[b]
        count[b] = slot + 1
        slot_of[r] = slot
        peer_row = b * (4 * PEER_ROWS)
        first[r] = peer_row
        shift = lon_shift[r]
        x = inc[r].astype(jnp.float32)
        half = [[x[f, 8 * h : 8 * h + 8] for h in range(2)] for f in range(4)]
        pieces = []
        for g in range(4):
            h, odd = g // 2, g % 2
            for f in (0, 2):
                upper, lower = half[f][h], half[f + 1][h]
                if odd:
                    upper = pltpu.roll(upper, 4, 0)
                else:
                    lower = pltpu.roll(lower, 4, 0)
                pieces.append(jnp.where(sub < 4, upper, lower))
        own = [None] * 8
        spill = [None] * 8
        for m in range(4):
            move = (shift + (m - 1 + 128)) & 127
            w = jnp.broadcast_to(weights[m, pl.ds(r, 1), :], (8, 128))
            w = pltpu.roll(w, move, 1)
            raw = lane - shift - (m - 1)
            inside = (raw >= 0) & (raw < 128)
            own_w = jnp.where(inside, w, 0.0)
            spill_w = jnp.where(inside, 0.0, w)
            for i in range(8):
                moved = pltpu.roll(pieces[i], move, 1)
                own[i] = own_w * moved if m == 0 else own[i] + own_w * moved
                spill[i] = spill_w * moved if m == 0 else spill[i] + spill_w * moved
        for i in range(8):
            stage[pl.ds(peer_row + (i // 2) * PEER_ROWS + slot * SLOT_ROWS + 8 * (i % 2), 8), :] = own[i]
            folded = jnp.where(lane < EDGE, spill[i] + pltpu.roll(spill[i], EDGE, 1), 0.0)
            edges[pl.ds(pl.multiple_of(r * 64 + 8 * i, 8), 8), :] = folded
        lat = lagrange(jnp.full((8, 128), lat_frac[r], jnp.float32))
        start = (tile_index[r] * TL + lat_offset[r]).astype(jnp.float32)
        meta = jnp.where(lane == META, start, jnp.where(lane == META + 1, shift.astype(jnp.float32), 0.0))
        for k in range(4):
            meta = jnp.where(lane == META + 2 + k, lat[k], meta)
        meta_lines[pl.ds(r, 1), :] = meta[0:1]
        return 0

    lax.fori_loop(0, rows, one_row, 0, unroll=4)

    for g in range(4):
        whole = meta_lines[...]
        rest = None
        for fl in range(SLOT_ROWS):
            line = edges[pl.ds(g * SLOT_ROWS + fl, rows, stride=64), :]
            if fl < WHOLE:
                whole = whole + (pltpu.roll(line, EDGE * fl, 1) if fl else line)
            else:
                line = pltpu.roll(line, EDGE * (fl - WHOLE), 1) if fl > WHOLE else line
                rest = line if rest is None else rest + line
        lines[2 * g] = whole
        lines[2 * g + 1] = rest

    def place(r, _):
        slot = slot_of[r]
        for g in range(4):
            at = first[r] + g * PEER_ROWS + OWN_ROWS
            stage[pl.ds(at + slot, 1), :] = lines[2 * g, pl.ds(r, 1), :]
            rest = jnp.broadcast_to(lines[2 * g + 1, pl.ds(r, 1), :], (8, 128))
            rest = pltpu.roll(rest, slot * (4 * EDGE), 1)
            stage[pl.ds(at + CAP, 1), :] = stage[pl.ds(at + CAP, 1), :] + rest[0:1]
        return 0

    lax.fori_loop(0, rows, place, 0, unroll=4)

    def finish(i, _):
        piece = pl.ds(pl.multiple_of(i * part, 16), part)
        out[piece, :] = stage[piece, :].astype(jnp.bfloat16)
        return 0

    lax.fori_loop(0, bands, finish, 0)


def tile_kernel(got, out, wide):
    peers = got.shape[0] // PEER_ROWS
    part = 4 * PEER_ROWS

    def widen(p, _):
        piece = pl.ds(pl.multiple_of(p * part, 16), part)
        wide[piece, :] = got[piece, :].astype(jnp.float32)
        return 0

    lax.fori_loop(0, peers // 4, widen, 0)

    def line_of_all(row):
        return wide[pl.ds(row, peers, stride=PEER_ROWS), :]

    lanes = lax.broadcasted_iota(jnp.int32, (peers, 128), 1)
    row_id = lanes.astype(jnp.float32)
    place = lanes % EDGE
    shared = line_of_all(OWN_ROWS + CAP)
    stencil, spill_next, spill_prev = [], [], []
    for j in range(CAP):
        line = line_of_all(OWN_ROWS + j)
        table = jnp.zeros((peers, 128), jnp.float32)
        start = line[:, META : META + 1]
        for k in range(4):
            table = table + jnp.where(row_id == start + float(k), line[:, META + 2 + k : META + 3 + k], 0.0)
        stencil.append(table.T.astype(jnp.bfloat16))
        shift = line[:, META + 1 : META + 2]
        forward = (shift > 0.5) | ((shift > -1.5) & (place < EDGE // 2))
        rest = pltpu.roll(shared, (128 - 4 * EDGE * j) % 128, 1) if j else shared
        both = [line, rest]
        spill_next.append(jnp.concatenate([jnp.where(forward, s, 0.0) for s in both], axis=1).astype(jnp.bfloat16))
        spill_prev.append(jnp.concatenate([jnp.where(forward, 0.0, s) for s in both], axis=1).astype(jnp.bfloat16))
    columns = jnp.concatenate(stencil, axis=1)

    def product(values):
        return jnp.dot(columns, jnp.concatenate(values, axis=0), preferred_element_type=jnp.float32)

    onward = product(spill_next)
    onward = jnp.concatenate([onward[128 - TL :], onward[: 128 - TL]], axis=0)
    back = product(spill_prev)
    back = jnp.concatenate([back[TL:], back[:TL]], axis=0)
    lane = lax.broadcasted_iota(jnp.int32, (128, 128), 1)
    for pair in range(8):
        values = []
        for j in range(CAP):
            cols = [line_of_all(j * SLOT_ROWS + 2 * pair + e).astype(jnp.bfloat16) for e in range(2)]
            values.append(jnp.concatenate(cols, axis=1))
        total = product(values)
        for e in range(2):
            fl = 2 * pair + e
            h, i = fl // WHOLE, fl % WHOLE
            ahead = pltpu.roll(onward[:, 128 * h : 128 * h + 128], (128 - EDGE * i) % 128, 1)
            behind = pltpu.roll(back[:, 128 * h : 128 * h + 128], (256 - EDGE - EDGE * i) % 128, 1)
            around = jnp.where(lane < EDGE, ahead, jnp.where(lane >= 128 - EDGE, behind, 0.0))
            out[fl % 4, fl // 4] = total[:, 128 * e : 128 * e + 128] + around


def local(increments, band, tile_index, lat_offset, lon_shift, lat_frac, lon_frac):
    rows = increments.shape[0]
    n_lat = lax.axis_size("lat")
    peers = 4 * n_lat
    hbm = pl.BlockSpec(memory_space=pltpu.HBM)
    vmem = pl.BlockSpec(memory_space=pltpu.VMEM)
    whole = (peers * PEER_ROWS, 128)
    send = pl.pallas_call(
        source_kernel,
        out_shape=jax.ShapeDtypeStruct(whole, jnp.bfloat16),
        in_specs=[hbm] * 7,
        out_specs=vmem,
        scratch_shapes=[pltpu.SMEM((rows,), jnp.int32)] * 4
        + [pltpu.SMEM((rows,), jnp.float32), pltpu.SMEM((n_lat,), jnp.int32)]
        + [pltpu.SMEM((rows,), jnp.int32)] * 2
        + [
            pltpu.VMEM(increments.shape, jnp.bfloat16),
            pltpu.VMEM((rows, 128), jnp.float32),
            pltpu.VMEM((4, rows, 128), jnp.float32),
            pltpu.VMEM(whole, jnp.float32),
            pltpu.VMEM((rows * 64, 128), jnp.float32),
            pltpu.VMEM((rows, 128), jnp.float32),
            pltpu.VMEM((8, rows, 128), jnp.float32),
            pltpu.SemaphoreType.DMA((7,)),
        ],
        compiler_params=pltpu.CompilerParams(vmem_limit_bytes=32 << 20),
        name="lon_slots",
    )(band.reshape(rows), tile_index, lat_offset, lon_shift, lat_frac, increments, lon_frac)
    fine = (peers * PEER_ROWS // 4, 4, 128)
    got = lax.all_to_all(send.reshape(fine), ("lat", "grp"), 0, 0, tiled=True)
    return pl.pallas_call(
        tile_kernel,
        out_shape=jax.ShapeDtypeStruct((4, 4, 128, 128), jnp.float32),
        in_specs=[vmem],
        out_specs=vmem,
        scratch_shapes=[pltpu.VMEM(whole, jnp.float32)],
        compiler_params=pltpu.CompilerParams(vmem_limit_bytes=40 << 20),
        name="tile_sums",
    )(got.reshape(whole))


def solution(mesh):
    in_specs = (
        P(("lat", "grp"), None, None, None),
        P(("lat", "grp"), None),
        P(("lat", "grp")),
        P(("lat", "grp")),
        P(("lat", "grp")),
        P(("lat", "grp")),
        P(("lat", "grp"), None),
    )
    out_specs = P("grp", None, "lat", None)
    return jax.shard_map(local, mesh=mesh, in_specs=in_specs, out_specs=out_specs, check_vma=False)
```

time: 131 us -> 117 us (0.89)
  Pallas kernels: 22.5 us -> 13.4 us
  blocking collectives: 103 us -> 98 us
    pallas_call x1, Pallas kernels: 17.3 us -> 9.35 us  [local(): pl.pallas_call(source_kernel, out_shape=jax.ShapeDtypeStruct(whole, jnp.b...]
    all_to_all x1, blocking collectives: 103 us -> 98 us  [local(): got = lax.all_to_all(send.reshape(fine), ('lat', 'grp'), 0, 0, tiled=True)]
where the time goes in v2:
time: 117 us
  blocking collectives  98 us (84%)
  Pallas kernels  13.4 us (11%)
  local copies, waits for them, and re-layouts  5.26 us (4%)
    all_to_all x1, blocking collectives, local(): got = lax.all_to_all(send.reshape(fine), ('lat', 'grp'), 0, 0, tiled=True)  98 us
    pallas_call x1, Pallas kernels, local(): pl.pallas_call(source_kernel, out_shape=jax.ShapeDtypeStruct(whole, jnp.b...  9.35 us
    unnamed x14, local copies, waits for them, and re-layouts  5.26 us
    pallas_call x1, Pallas kernels, local(): pl.pallas_call(tile_kernel, out_shape=jax.ShapeDtypeStruct((4, 4, 128, 12...  4.04 us

profile of v2, /device:TPU:1, one launch (start us, length us, event | category | flops | bytes accessed | tf_op | source)
XLA Modules:
  0.0 116.6 jit_solution(17955577633931071535)
XLA Ops:
  0.0 0.0 copy-start
  0.0 1.2 %copy-done = bf16[64,4,16,128]{3,2,1,0:T(8,128)(2,1)S(1)} copy-done((bf16[64,4,16,128]{3,2,1,0:T(8,128)(2,1)S(1)}, bf16[64,4,16,128]{3,2,1,0:T(8,128)(2,1)}, u32[]{:S(2)}) %copy-start) | copy-done | bytes 1048600
  1.2 0.0 copy-start.1
  1.2 0.8 copy-done.1
  2.0 0.0 copy-start.2
  2.0 0.7 copy-done.2
  2.6 0.0 copy-start.3
  2.6 0.7 copy-done.3
  3.3 0.0 copy-start.4
  3.3 0.7 copy-done.4
  4.0 0.0 copy-start.5
  4.0 0.7 copy-done.5
  4.6 0.0 copy-start.6
  4.6 0.7 copy-done.6
  5.3 9.3 %lon_slots.1 = bf16[13312,128]{1,0:T(8,128)(2,1)S(1)} custom-call(s32[64]{0:T(128)S(1)} %bitcast.5, s32[64]{0:T(128)S(1)} %copy-done.3, s32[64]{0:T(128)S(1)} %copy-done.4, s32[64]{0:T(128)S(1)} %copy-done.5, f32[64]{0:T(128)S(1)} %copy-done.6, bf16[64,4,16,128]{3,2,1,0:T(8,128)(2,1)S(1)} %copy-done, f32[64,128]{1,0:T(8,128)S(1)} %copy-done.1), custom_call_target="tpu_custom_call" | custom-call | tf_op jit(solution)/shard_map/lon_slots/pallas_call | solution.py:208
  14.6 98.0 %all_to_all.5 = bf16[3328,4,128]{2,1,0:T(4,128)(2,1)S(1)} all-to-all(bf16[3328,4,128]{2,1,0:T(4,128)(2,1)S(1)} %bitcast.4), channel_id=1, replica_groups=mesh['lat'=64,'grp'=4] {'lat','grp'}, dimensions={0} | all-to-all | bytes 6815744 | tf_op jit(solution)/shard_map/all_to_all | solution.py:230
  112.6 4.0 %tile_sums.1 = f32[4,4,128,128]{3,2,1,0:T(8,128)} custom-call(bf16[13312,128]{1,0:T(8,128)(2,1)S(1)} %bitcast.3), custom_call_target="tpu_custom_call" | custom-call | tf_op jit(solution)/shard_map/tile_sums/pallas_call | solution.py:231
Async XLA Ops:
  0.0 1.2 %copy-start = (bf16[64,4,16,128]{3,2,1,0:T(8,128)(2,1)S(1)}, bf16[64,4,16,128]{3,2,1,0:T(8,128)(2,1)}, u32[]{:S(2)}) copy-start(bf16[64,4,16,128]{3,2,1,0:T(8,128)(2,1)} %inc_hbm.1) | copy-start | bytes 3145732
  1.2 0.8 copy-start.1
  2.0 0.7 copy-start.2
  2.6 0.7 copy-start.3
  3.3 0.7 copy-start.4
  4.0 0.7 copy-start.5
  4.6 0.7 copy-start.6

commit v3 on v2

--- a/solution.py
+++ b/solution.py
@@ -223,7 +223,7 @@
             pltpu.VMEM((8, rows, 128), jnp.float32),
             pltpu.SemaphoreType.DMA((7,)),
         ],
-        compiler_params=pltpu.CompilerParams(vmem_limit_bytes=32 << 20),
+        compiler_params=pltpu.CompilerParams(vmem_limit_bytes=60 << 20),
         name="lon_slots",
     )(band.reshape(rows), tile_index, lat_offset, lon_shift, lat_frac, increments, lon_frac)
     fine = (peers * PEER_ROWS // 4, 4, 128)

time: 117 us -> 114 us (0.974)
  local copies, waits for them, and re-layouts: 5.26 us -> 0 us
  Pallas kernels: 13.4 us -> 15.7 us
    unnamed x14 -> x0, local copies, waits for them, and re-layouts: 5.26 us -> none
    pallas_call x1, Pallas kernels: 9.35 us -> 11.7 us  [local(): pl.pallas_call(source_kernel, out_shape=jax.ShapeDtypeStruct(whole, jnp.b...]
where the time goes in v3:
time: 114 us
  blocking collectives  98.2 us (86%)
  Pallas kernels  15.7 us (14%)
    all_to_all x1, blocking collectives, local(): got = lax.all_to_all(send.reshape(fine), ('lat', 'grp'), 0, 0, tiled=True)  98.2 us
    pallas_call x1, Pallas kernels, local(): pl.pallas_call(source_kernel, out_shape=jax.ShapeDtypeStruct(whole, jnp.b...  11.7 us
    pallas_call x1, Pallas kernels, local(): pl.pallas_call(tile_kernel, out_shape=jax.ShapeDtypeStruct((4, 4, 128, 12...  4.04 us

profile of v3, /device:TPU:1, one launch (start us, length us, event | category | flops | bytes accessed | tf_op | source)
XLA Modules:
  0.0 113.9 jit_solution(9497788409165291856)
XLA Ops:
  0.0 11.7 %lon_slots.1 = bf16[13312,128]{1,0:T(8,128)(2,1)} custom-call(s32[64]{0:T(128)} %bitcast.5, s32[64]{0:T(128)} %tile_hbm.1, s32[64]{0:T(128)} %offset_hbm.1, s32[64]{0:T(128)} %shift_hbm.1, f32[64]{0:T(128)} %lat_hbm.1, bf16[64,4,16,128]{3,2,1,0:T(8,128)(2,1)} %inc_hbm.1, f32[64,128]{1,0:T(8,128)} %lon_hbm.1), custom_call_target="tpu_custom_call" | custom-call | tf_op jit(solution)/shard_map/lon_slots/pallas_call | solution.py:208
  11.7 98.2 %all_to_all.5 = bf16[3328,4,128]{2,1,0:T(4,128)(2,1)S(1)} all-to-all(bf16[3328,4,128]{2,1,0:T(4,128)(2,1)} %bitcast.4), channel_id=1, replica_groups=mesh['lat'=64,'grp'=4] {'lat','grp'}, dimensions={0} | all-to-all | bytes 6815744 | tf_op jit(solution)/shard_map/all_to_all | solution.py:230
  109.9 4.0 %tile_sums.1 = f32[4,4,128,128]{3,2,1,0:T(8,128)} custom-call(bf16[13312,128]{1,0:T(8,128)(2,1)S(1)} %bitcast.3), custom_call_target="tpu_custom_call" | custom-call | tf_op jit(solution)/shard_map/tile_sums/pallas_call | solution.py:231

commit v4 on v3

--- a/solution.py
+++ b/solution.py
@@ -13,6 +13,8 @@
 EDGE = 10
 WHOLE = 12
 META = EDGE * WHOLE
+PITCH = 65
+OUT_PARTS = 8
 
 
 def lagrange(fraction):
@@ -31,7 +33,7 @@
 def source_kernel(
     band_hbm, tile_hbm, offset_hbm, shift_hbm, lat_hbm, inc_hbm, lon_hbm, out,
     band, tile_index, lat_offset, lon_shift, lat_frac, count, first, slot_of,
-    inc, lon_frac, weights, stage, edges, meta_lines, lines, sems,
+    inc, lon_frac, weights, stage, packed, edges, meta_lines, lines, rests, sems, out_sems,
 ):
     rows = inc.shape[0]
     bands = count.shape[0]
@@ -96,49 +98,68 @@
                 spill[i] = spill_w * moved if m == 0 else spill[i] + spill_w * moved
         for i in range(8):
             stage[pl.ds(peer_row + (i // 2) * PEER_ROWS + slot * SLOT_ROWS + 8 * (i % 2), 8), :] = own[i]
-            folded = jnp.where(lane < EDGE, spill[i] + pltpu.roll(spill[i], EDGE, 1), 0.0)
-            edges[pl.ds(pl.multiple_of(r * 64 + 8 * i, 8), 8), :] = folded
-        lat = lagrange(jnp.full((8, 128), lat_frac[r], jnp.float32))
+            edges[pl.ds(r * PITCH + 8 * i, 8), :] = spill[i]
         start = (tile_index[r] * TL + lat_offset[r]).astype(jnp.float32)
         meta = jnp.where(lane == META, start, jnp.where(lane == META + 1, shift.astype(jnp.float32), 0.0))
-        for k in range(4):
-            meta = jnp.where(lane == META + 2 + k, lat[k], meta)
+        meta = jnp.where(lane > META + 1, lat_frac[r], meta)
         meta_lines[pl.ds(r, 1), :] = meta[0:1]
         return 0
 
     lax.fori_loop(0, rows, one_row, 0, unroll=4)
 
-    for g in range(4):
-        whole = meta_lines[...]
-        rest = None
-        for fl in range(SLOT_ROWS):
-            line = edges[pl.ds(g * SLOT_ROWS + fl, rows, stride=64), :]
-            if fl < WHOLE:
-                whole = whole + (pltpu.roll(line, EDGE * fl, 1) if fl else line)
-            else:
-                line = pltpu.roll(line, EDGE * (fl - WHOLE), 1) if fl > WHOLE else line
-                rest = line if rest is None else rest + line
-        lines[2 * g] = whole
-        lines[2 * g + 1] = rest
+    def pack(n, _):
+        rows_here = pl.ds(pl.multiple_of(8 * n, 8), 8)
+        meta = meta_lines[rows_here, :]
+        for k, w in enumerate(lagrange(meta)):
+            meta = jnp.where(lane == META + 2 + k, w, meta)
+        meta = jnp.where(lane < META + 6, meta, 0.0)
+        for g in range(4):
+            whole = meta
+            rest = None
+            for fl in range(SLOT_ROWS):
+                line = edges[pl.ds(n * (8 * PITCH) + g * SLOT_ROWS + fl, 8, stride=PITCH), :]
+                line = jnp.where(lane < EDGE, line + pltpu.roll(line, EDGE, 1), 0.0)
+                if fl < WHOLE:
+                    whole = whole + (pltpu.roll(line, EDGE * fl, 1) if fl else line)
+                else:
+                    line = pltpu.roll(line, EDGE * (fl - WHOLE), 1) if fl > WHOLE else line
+                    rest = line if rest is None else rest + line
+            lines[g, rows_here, :] = whole
+            for slot in range(CAP):
+                lines[4 + CAP * g + slot, rows_here, :] = pltpu.roll(rest, 4 * EDGE * slot, 1) if slot else rest
+        return 0
+
+    lax.fori_loop(0, rows // 8, pack, 0)
+    rests[...] = jnp.zeros(rests.shape, jnp.float32)
 
     def place(r, _):
         slot = slot_of[r]
+        row = pl.ds(r, 1)
+        at = first[r] + OWN_ROWS + slot
+        peer = band[r] * 4
         for g in range(4):
-            at = first[r] + g * PEER_ROWS + OWN_ROWS
-            stage[pl.ds(at + slot, 1), :] = lines[2 * g, pl.ds(r, 1), :]
-            rest = jnp.broadcast_to(lines[2 * g + 1, pl.ds(r, 1), :], (8, 128))
-            rest = pltpu.roll(rest, slot * (4 * EDGE), 1)
-            stage[pl.ds(at + CAP, 1), :] = stage[pl.ds(at + CAP, 1), :] + rest[0:1]
-        return 0
-
-    lax.fori_loop(0, rows, place, 0, unroll=4)
-
-    def finish(i, _):
-        piece = pl.ds(pl.multiple_of(i * part, 16), part)
-        out[piece, :] = stage[piece, :].astype(jnp.bfloat16)
-        return 0
-
-    lax.fori_loop(0, bands, finish, 0)
+            stage[pl.ds(at + g * PEER_ROWS, 1), :] = lines[g, row, :]
+            rests[slot, pl.ds(peer + g, 1), :] = lines[4 + CAP * g + slot, row, :]
+        return 0
+
+    lax.fori_loop(0, rows, place, 0, unroll=8)
+    stage[pl.ds(OWN_ROWS + CAP, 4 * bands, stride=PEER_ROWS), :] = rests[0] + rests[1] + rests[2]
+
+    size = stage.shape[0] // OUT_PARTS
+    sends = []
+    for n in range(OUT_PARTS):
+
+        def finish(i, _):
+            piece = pl.ds(pl.multiple_of(n * size + i * part, 16), part)
+            packed[piece, :] = stage[piece, :].astype(jnp.bfloat16)
+            return 0
+
+        lax.fori_loop(0, bands // OUT_PARTS, finish, 0)
+        span = pl.ds(n * size, size)
+        sends.append(pltpu.make_async_copy(packed.at[span, :], out.at[span, :], out_sems.at[n]))
+        sends[-1].start()
+    for send in sends:
+        send.wait()
 
 
 def tile_kernel(got, out, wide):
@@ -209,7 +230,7 @@
         source_kernel,
         out_shape=jax.ShapeDtypeStruct(whole, jnp.bfloat16),
         in_specs=[hbm] * 7,
-        out_specs=vmem,
+        out_specs=hbm,
         scratch_shapes=[pltpu.SMEM((rows,), jnp.int32)] * 4
         + [pltpu.SMEM((rows,), jnp.float32), pltpu.SMEM((n_lat,), jnp.int32)]
         + [pltpu.SMEM((rows,), jnp.int32)] * 2
@@ -218,10 +239,13 @@
             pltpu.VMEM((rows, 128), jnp.float32),
             pltpu.VMEM((4, rows, 128), jnp.float32),
             pltpu.VMEM(whole, jnp.float32),
-            pltpu.VMEM((rows * 64, 128), jnp.float32),
+            pltpu.VMEM(whole, jnp.bfloat16),
+            pltpu.VMEM((rows * PITCH, 128), jnp.float32),
             pltpu.VMEM((rows, 128), jnp.float32),
-            pltpu.VMEM((8, rows, 128), jnp.float32),
+            pltpu.VMEM((4 + 4 * CAP, rows, 128), jnp.float32),
+            pltpu.VMEM((CAP, peers, 128), jnp.float32),
             pltpu.SemaphoreType.DMA((7,)),
+            pltpu.SemaphoreType.DMA((OUT_PARTS,)),
         ],
         compiler_params=pltpu.CompilerParams(vmem_limit_bytes=60 << 20),
         name="lon_slots",

time: 114 us -> 111 us (0.974)
  Pallas kernels: 15.7 us -> 12.2 us
    pallas_call x1, Pallas kernels: 11.7 us -> 8.19 us  [local(): pl.pallas_call(source_kernel, out_shape=jax.ShapeDtypeStruct(whole, jnp.b...]
where the time goes in v4:
time: 111 us; the launch traced here: 110 us
  blocking collectives  98.2 us (88%)
  Pallas kernels  12.2 us (11%)
    all_to_all x1, blocking collectives, local(): got = lax.all_to_all(send.reshape(fine), ('lat', 'grp'), 0, 0, tiled=True)  98.2 us
    pallas_call x1, Pallas kernels, local(): pl.pallas_call(source_kernel, out_shape=jax.ShapeDtypeStruct(whole, jnp.b...  8.19 us
    pallas_call x1, Pallas kernels, local(): pl.pallas_call(tile_kernel, out_shape=jax.ShapeDtypeStruct((4, 4, 128, 12...  4.04 us

profile of v4, /device:TPU:1, one launch (start us, length us, event | category | flops | bytes accessed | tf_op | source)
XLA Modules:
  0.0 110.4 jit_solution(9925967054911692228)
XLA Ops:
  0.0 8.2 %lon_slots.1 = bf16[13312,128]{1,0:T(8,128)(2,1)} custom-call(s32[64]{0:T(128)} %bitcast.5, s32[64]{0:T(128)} %tile_hbm.1, s32[64]{0:T(128)} %offset_hbm.1, s32[64]{0:T(128)} %shift_hbm.1, f32[64]{0:T(128)} %lat_hbm.1, bf16[64,4,16,128]{3,2,1,0:T(8,128)(2,1)} %inc_hbm.1, f32[64,128]{1,0:T(8,128)} %lon_hbm.1), custom_call_target="tpu_custom_call" | custom-call | tf_op jit(solution)/shard_map/lon_slots/pallas_call | solution.py:229
  8.2 98.2 %all_to_all.5 = bf16[3328,4,128]{2,1,0:T(4,128)(2,1)S(1)} all-to-all(bf16[3328,4,128]{2,1,0:T(4,128)(2,1)} %bitcast.4), channel_id=1, replica_groups=mesh['lat'=64,'grp'=4] {'lat','grp'}, dimensions={0} | all-to-all | bytes 6815744 | tf_op jit(solution)/shard_map/all_to_all | solution.py:254
  106.4 4.0 %tile_sums.1 = f32[4,4,128,128]{3,2,1,0:T(8,128)} custom-call(bf16[13312,128]{1,0:T(8,128)(2,1)S(1)} %bitcast.3), custom_call_target="tpu_custom_call" | custom-call | tf_op jit(solution)/shard_map/tile_sums/pallas_call | solution.py:255

commit v5 on v4

v5 whole, which is shorter than its diff:
```python
import jax
import jax.numpy as jnp
from jax import lax
from jax.experimental import pallas as pl
from jax.experimental.pallas import tpu as pltpu
from jax.sharding import PartitionSpec as P

TL = 16
CAP = 3
SLOT_ROWS = 16
OWN_ROWS = CAP * SLOT_ROWS
PEER_ROWS = OWN_ROWS + 2
OVER = 3
META = OVER * SLOT_ROWS
FIELD = 16
PITCH = 65
OUT_PARTS = 8
SPARE = 72


def lagrange(fraction):
    return [
        -fraction * (fraction - 1.0) * (fraction - 2.0) / 6.0,
        (fraction + 1.0) * (fraction - 1.0) * (fraction - 2.0) / 2.0,
        -(fraction + 1.0) * fraction * (fraction - 2.0) / 2.0,
        (fraction + 1.0) * fraction * (fraction - 1.0) / 6.0,
    ]


def rounded(x):
    return x.astype(jnp.bfloat16).astype(jnp.float32)


def source_kernel(
    band_hbm, tile_hbm, offset_hbm, shift_hbm, lat_hbm, inc_hbm, lon_hbm, out,
    band, tile_index, lat_offset, lon_shift, lat_frac, count, slot_of,
    inc, lon_frac, weights, stage, packed, edges, meta_lines, lines, rests, sems, out_sems,
):
    rows = inc.shape[0]
    bands = count.shape[0]
    pairs = (
        (band_hbm, band), (tile_hbm, tile_index), (offset_hbm, lat_offset), (shift_hbm, lon_shift),
        (lat_hbm, lat_frac), (lon_hbm, lon_frac), (inc_hbm, inc),
    )
    copies = [pltpu.make_async_copy(src, dst, sems.at[i]) for i, (src, dst) in enumerate(pairs)]
    for copy in copies:
        copy.start()

    lane = lax.broadcasted_iota(jnp.int32, (8, 128), 1)
    sub = lax.broadcasted_iota(jnp.int32, (8, 128), 0)
    zero = jnp.zeros((8, 128), jnp.float32)
    part = out.shape[0] // (bands // 2)

    def clear(i, _):
        stage[pl.ds(pl.multiple_of(i * part, 8), part), :] = jnp.zeros((part, 128), jnp.float32)
        count[2 * i] = 0
        count[2 * i + 1] = 0
        return 0

    lax.fori_loop(0, bands // 2, clear, 0)
    rests[...] = jnp.zeros(rests.shape, jnp.float32)
    for copy in copies:
        copy.wait()

    for m, w in enumerate(lagrange(lon_frac[...])):
        weights[m] = rounded(w)

    def one_row(r, _):
        b = band[r]
        slot = count[b]
        count[b] = slot + 1
        slot_of[r] = slot
        peer_row = b * (4 * PEER_ROWS)
        shift = lon_shift[r]
        x = inc[r].astype(jnp.float32)
        pieces = [x[i // 2, 8 * (i % 2) : 8 * (i % 2) + 8] for i in range(8)]
        own = [None] * 8
        over = [None] * 8
        for m in range(4):
            move = (shift + (m - 1 + 128)) & 127
            w = jnp.broadcast_to(weights[m, pl.ds(r, 1), :], (8, 128))
            w = pltpu.roll(w, move, 1)
            inside = ((lane - shift - (m - 1)) & 127) < 128 - m
            own_w = jnp.where(inside, w, 0.0)
            over_w = jnp.where(inside, 0.0, w)
            for i in range(8):
                moved = pltpu.roll(pieces[i], move, 1)
                own[i] = own_w * moved if m == 0 else own[i] + own_w * moved
                if m > 0:
                    over[i] = over_w * moved if m == 1 else over[i] + over_w * moved
        at = peer_row + slot * SLOT_ROWS
        for i in range(8):
            f, h = i // 2, i % 2
            low = pl.ds(at + 2 * h * PEER_ROWS + 4 * f, 8)
            pltpu.store(stage.at[low, :], own[i], mask=sub < 4)
            high = pl.ds(at + (2 * h + 1) * PEER_ROWS + 4 * f - 4, 8)
            pltpu.store(stage.at[high, :], own[i], mask=sub >= 4)
            edges[pl.ds(r * PITCH + 8 * i, 8), :] = over[i]
        start = (tile_index[r] * TL + lat_offset[r]).astype(jnp.float32)
        meta = jnp.where(lane == META, start, jnp.where(lane == META + 1, shift.astype(jnp.float32), 0.0))
        meta = jnp.where(lane > META + 1, lat_frac[r], meta)
        meta_lines[pl.ds(r, 1), :] = meta[0:1]
        return 0

    lax.fori_loop(0, rows, one_row, 0, unroll=8)

    def align(r, _):
        back = (129 - lon_shift[r]) & 127
        for i in range(8):
            piece = pl.ds(r * PITCH + 8 * i, 8)
            edges[piece, :] = pltpu.roll(edges[piece, :], back, 1)
        return 0

    lax.fori_loop(0, rows, align, 0, unroll=8)

    def pack(n, _):
        rows_here = pl.ds(pl.multiple_of(8 * n, 8), 8)
        meta = meta_lines[rows_here, :]
        for k, w in enumerate(lagrange(meta)):
            meta = jnp.where(lane == META + 2 + k, w, meta)
        meta = jnp.where((lane >= META) & (lane < META + 6), meta, 0.0)
        for g in range(4):
            whole = meta
            for fl in range(SLOT_ROWS):
                line = edges[pl.ds(n * (8 * PITCH) + (fl // 4) * 16 + 4 * g + fl % 4, 8, stride=PITCH), :]
                whole = whole + (pltpu.roll(line, OVER * fl, 1) if fl else line)
            lines[g, rows_here, :] = whole
            lines[4 + g, rows_here, :] = pltpu.roll(whole, 64, 1)
        return 0

    lax.fori_loop(0, rows // 8, pack, 0)

    def place(r, _):
        slot = slot_of[r]
        row = pl.ds(r, 1)
        peer = band[r] * 4
        side = jnp.where(slot == 1, 4, 0)
        for g in range(4):
            rests[slot, pl.ds(peer + g, 1), :] = lines[side + g, row, :]
        return 0

    lax.fori_loop(0, rows, place, 0, unroll=8)
    stage[pl.ds(OWN_ROWS, 4 * bands, stride=PEER_ROWS), :] = rests[0] + rests[1]
    stage[pl.ds(OWN_ROWS + 1, 4 * bands, stride=PEER_ROWS), :] = rests[2]

    size = out.shape[0] // OUT_PARTS
    sends = []
    for n in range(OUT_PARTS):

        def finish(i, _):
            piece = pl.ds(pl.multiple_of(n * size + i * part, 16), part)
            packed[piece, :] = stage[piece, :].astype(jnp.bfloat16)
            return 0

        lax.fori_loop(0, bands // (2 * OUT_PARTS), finish, 0)
        span = pl.ds(n * size, size)
        sends.append(pltpu.make_async_copy(packed.at[span, :], out.at[span, :], out_sems.at[n]))
        sends[-1].start()
    for send in sends:
        send.wait()


def tile_kernel(got, out, wide, result, sems):
    peers = got.shape[0] // PEER_ROWS
    part = 8 * PEER_ROWS

    def widen(p, _):
        piece = pl.ds(pl.multiple_of(p * part, 16), part)
        wide[piece, :] = got[piece, :].astype(jnp.float32)
        return 0

    lax.fori_loop(0, peers // 8, widen, 0)

    def line_of_all(row):
        return wide[pl.ds(row, peers, stride=PEER_ROWS), :]

    lanes = lax.broadcasted_iota(jnp.int32, (peers, 128), 1)
    row_id = lanes.astype(jnp.float32)
    field, place = lanes // FIELD, lanes % FIELD
    pair_line = line_of_all(OWN_ROWS)
    slot_lines = [pair_line, pltpu.roll(pair_line, 64, 1), line_of_all(OWN_ROWS + 1)]
    stencil, here, over_next, over_own = [], [], [], []
    for line in slot_lines:
        table = jnp.zeros((peers, 128), jnp.float32)
        start = line[:, META : META + 1]
        for k in range(4):
            table = table + jnp.where(row_id == start + float(k), line[:, META + 2 + k : META + 3 + k], 0.0)
        stencil.append(table.T.astype(jnp.bfloat16))
        shift = jnp.broadcast_to(line[:, META + 1 : META + 2], (peers, 128)).astype(jnp.int32)
        step = lanes - shift
        mask = jnp.where((step >= -1) & (step <= 126), 1.0, 0.0).astype(jnp.bfloat16)
        here.append(jnp.concatenate([mask, mask], axis=1))
        ahead = place - shift + 1
        local_e = ahead - FIELD
        is_next = (ahead >= 0) & (ahead <= 2)
        is_own = (local_e >= 0) & (local_e <= 2)
        column = jnp.where(is_own, local_e, jnp.where(is_next, ahead, 0))
        nexts, owns = [], []
        for h in range(2):
            picked = jnp.take_along_axis(line, column + OVER * (field + 8 * h), axis=1)
            nexts.append(jnp.where(is_next, picked, 0.0))
            owns.append(jnp.where(is_own, picked, 0.0))
        over_next.append(jnp.concatenate(nexts, axis=1).astype(jnp.bfloat16))
        over_own.append(jnp.concatenate(owns, axis=1).astype(jnp.bfloat16))
    columns = jnp.concatenate(stencil, axis=1)
    here = jnp.concatenate(here, axis=0)

    def product(values):
        return jnp.dot(columns, values, preferred_element_type=jnp.float32)

    def later(x):
        return jnp.concatenate([x[128 - TL :], x[: 128 - TL]], axis=0)

    def earlier(x):
        return jnp.concatenate([x[TL:], x[:TL]], axis=0)

    onward = later(product(jnp.concatenate(over_next, axis=0)))
    local_over = product(jnp.concatenate(over_own, axis=0))
    lane = lax.broadcasted_iota(jnp.int32, (128, 128), 1)
    sends = []
    for pair in range(8):
        values = []
        for j in range(CAP):
            cols = [line_of_all(j * SLOT_ROWS + 2 * pair + e).astype(jnp.bfloat16) for e in range(2)]
            values.append(jnp.concatenate(cols, axis=1))
        values = jnp.concatenate(values, axis=0)
        staying = values * here
        total = product(staying)
        moving = product(values - staying)
        for e in range(2):
            fl = 2 * pair + e
            h, i = fl // 8, fl % 8
            ahead = pltpu.roll(onward[:, 128 * h : 128 * h + 128], (128 - FIELD * i) % 128, 1)
            behind = pltpu.roll(local_over[:, 128 * h : 128 * h + 128], (256 - FIELD - FIELD * i) % 128, 1)
            around = jnp.where(lane < FIELD, ahead, jnp.where(lane >= 128 - FIELD, behind, 0.0))
            part_moving = moving[:, 128 * e : 128 * e + 128]
            around = around + jnp.where(lane < 64, later(part_moving), earlier(part_moving))
            spot = (fl % 4, fl // 4)
            result[spot] = total[:, 128 * e : 128 * e + 128] + around
            sends.append(pltpu.make_async_copy(result.at[spot], out.at[spot], sems.at[fl]))
            sends[-1].start()
    for send in sends:
        send.wait()


def local(increments, band, tile_index, lat_offset, lon_shift, lat_frac, lon_frac):
    rows = increments.shape[0]
    n_lat = lax.axis_size("lat")
    peers = 4 * n_lat
    hbm = pl.BlockSpec(memory_space=pltpu.HBM)
    vmem = pl.BlockSpec(memory_space=pltpu.VMEM)
    whole = (peers * PEER_ROWS, 128)
    roomy = (peers * PEER_ROWS + SPARE, 128)
    send = pl.pallas_call(
        source_kernel,
        out_shape=jax.ShapeDtypeStruct(whole, jnp.bfloat16),
        in_specs=[hbm] * 7,
        out_specs=hbm,
        scratch_shapes=[pltpu.SMEM((rows,), jnp.int32)] * 4
        + [pltpu.SMEM((rows,), jnp.float32), pltpu.SMEM((n_lat,), jnp.int32)]
        + [pltpu.SMEM((rows,), jnp.int32)]
        + [
            pltpu.VMEM(increments.shape, jnp.bfloat16),
            pltpu.VMEM((rows, 128), jnp.float32),
            pltpu.VMEM((4, rows, 128), jnp.float32),
            pltpu.VMEM(roomy, jnp.float32),
            pltpu.VMEM(whole, jnp.bfloat16),
            pltpu.VMEM((rows * PITCH + SPARE, 128), jnp.float32),
            pltpu.VMEM((rows, 128), jnp.float32),
            pltpu.VMEM((8, rows, 128), jnp.float32),
            pltpu.VMEM((CAP, peers, 128), jnp.float32),
            pltpu.SemaphoreType.DMA((7,)),
            pltpu.SemaphoreType.DMA((OUT_PARTS,)),
        ],
        compiler_params=pltpu.CompilerParams(vmem_limit_bytes=60 << 20),
        name="lon_slots",
    )(band.reshape(rows), tile_index, lat_offset, lon_shift, lat_frac, increments, lon_frac)
    fine = (peers * PEER_ROWS // 2, 2, 128)
    got = lax.all_to_all(send.reshape(fine), ("lat", "grp"), 0, 0, tiled=True)
    return pl.pallas_call(
        tile_kernel,
        out_shape=jax.ShapeDtypeStruct((4, 4, 128, 128), jnp.float32),
        in_specs=[vmem],
        out_specs=hbm,
        scratch_shapes=[
            pltpu.VMEM(roomy, jnp.float32),
            pltpu.VMEM((4, 4, 128, 128), jnp.float32),
            pltpu.SemaphoreType.DMA((SLOT_ROWS,)),
        ],
        compiler_params=pltpu.CompilerParams(vmem_limit_bytes=40 << 20),
        name="tile_sums",
    )(got.reshape(whole))


def solution(mesh):
    in_specs = (
        P(("lat", "grp"), None, None, None),
        P(("lat", "grp"), None),
        P(("lat", "grp")),
        P(("lat", "grp")),
        P(("lat", "grp")),
        P(("lat", "grp")),
        P(("lat", "grp"), None),
    )
    out_specs = P("grp", None, "lat", None)
    return jax.shard_map(local, mesh=mesh, in_specs=in_specs, out_specs=out_specs, check_vma=False)
```

time: 111 us -> 108 us (0.973)
  blocking collectives: 98.2 us -> 95.4 us
    all_to_all x1, blocking collectives: 98.2 us -> 95.4 us  [local(): got = lax.all_to_all(send.reshape(fine), ('lat', 'grp'), 0, 0, tiled=True)]
where the time goes in v5:
time: 108 us
  blocking collectives  95.4 us (88%)
  Pallas kernels  12.4 us (11%)
    all_to_all x1, blocking collectives, local(): got = lax.all_to_all(send.reshape(fine), ('lat', 'grp'), 0, 0, tiled=True)  95.4 us
    pallas_call x1, Pallas kernels, local(): pl.pallas_call(source_kernel, out_shape=jax.ShapeDtypeStruct(whole, jnp.b...  8.08 us
    pallas_call x1, Pallas kernels, local(): pl.pallas_call(tile_kernel, out_shape=jax.ShapeDtypeStruct((4, 4, 128, 12...  4.29 us

profile of v5, /device:TPU:1, one launch (start us, length us, event | category | flops | bytes accessed | tf_op | source)
XLA Modules:
  0.0 107.8 jit_solution(956660620628060137)
XLA Ops:
  0.0 8.1 %lon_slots.1 = bf16[12800,128]{1,0:T(8,128)(2,1)} custom-call(s32[64]{0:T(128)} %bitcast.5, s32[64]{0:T(128)} %tile_hbm.1, s32[64]{0:T(128)} %offset_hbm.1, s32[64]{0:T(128)} %shift_hbm.1, f32[64]{0:T(128)} %lat_hbm.1, bf16[64,4,16,128]{3,2,1,0:T(8,128)(2,1)} %inc_hbm.1, f32[64,128]{1,0:T(8,128)} %lon_hbm.1), custom_call_target="tpu_custom_call" | custom-call | tf_op jit(solution)/shard_map/lon_slots/pallas_call | solution.py:254
  8.1 95.4 %all_to_all.5 = bf16[6400,2,128]{2,1,0:T(2,128)(2,1)S(1)} all-to-all(bf16[6400,2,128]{2,1,0:T(2,128)(2,1)} %bitcast.4), channel_id=1, replica_groups=mesh['lat'=64,'grp'=4] {'lat','grp'}, dimensions={0} | all-to-all | bytes 6553600 | tf_op jit(solution)/shard_map/all_to_all | solution.py:279
  103.5 4.3 %tile_sums.1 = f32[4,4,128,128]{3,2,1,0:T(8,128)} custom-call(bf16[12800,128]{1,0:T(8,128)(2,1)S(1)} %bitcast.3), custom_call_target="tpu_custom_call" | custom-call | tf_op jit(solution)/shard_map/tile_sums/pallas_call | solution.py:280

commit v6 on v5

--- a/solution.py
+++ b/solution.py
@@ -40,8 +40,9 @@
     bands = count.shape[0]
     pairs = (
         (band_hbm, band), (tile_hbm, tile_index), (offset_hbm, lat_offset), (shift_hbm, lon_shift),
-        (lat_hbm, lat_frac), (lon_hbm, lon_frac), (inc_hbm, inc),
+        (lat_hbm, lat_frac),
     )
+    pairs = ((inc_hbm, inc), (lon_hbm, lon_frac)) + pairs
     copies = [pltpu.make_async_copy(src, dst, sems.at[i]) for i, (src, dst) in enumerate(pairs)]
     for copy in copies:
         copy.start()
@@ -59,11 +60,14 @@
 
     lax.fori_loop(0, bands // 2, clear, 0)
     rests[...] = jnp.zeros(rests.shape, jnp.float32)
-    for copy in copies:
-        copy.wait()
+    copies[1].wait()
 
     for m, w in enumerate(lagrange(lon_frac[...])):
         weights[m] = rounded(w)
+
+    for copy in copies[2:]:
+        copy.wait()
+    copies[0].wait()
 
     def one_row(r, _):
         b = band[r]
@@ -102,20 +106,13 @@
         meta_lines[pl.ds(r, 1), :] = meta[0:1]
         return 0
 
-    lax.fori_loop(0, rows, one_row, 0, unroll=8)
-
-    def align(r, _):
-        back = (129 - lon_shift[r]) & 127
-        for i in range(8):
-            piece = pl.ds(r * PITCH + 8 * i, 8)
-            edges[piece, :] = pltpu.roll(edges[piece, :], back, 1)
-        return 0
-
-    lax.fori_loop(0, rows, align, 0, unroll=8)
+    lax.fori_loop(0, rows, one_row, 0, unroll=16)
 
     def pack(n, _):
         rows_here = pl.ds(pl.multiple_of(8 * n, 8), 8)
         meta = meta_lines[rows_here, :]
+        shift = jnp.broadcast_to(meta[:, META + 1 : META + 2], (8, 128)).astype(jnp.int32)
+        origin = (shift + 127 + lane % OVER) & 127
         for k, w in enumerate(lagrange(meta)):
             meta = jnp.where(lane == META + 2 + k, w, meta)
         meta = jnp.where((lane >= META) & (lane < META + 6), meta, 0.0)
@@ -123,12 +120,12 @@
             whole = meta
             for fl in range(SLOT_ROWS):
                 line = edges[pl.ds(n * (8 * PITCH) + (fl // 4) * 16 + 4 * g + fl % 4, 8, stride=PITCH), :]
-                whole = whole + (pltpu.roll(line, OVER * fl, 1) if fl else line)
+                whole = jnp.where(lane // OVER == fl, jnp.take_along_axis(line, origin, axis=1), whole)
             lines[g, rows_here, :] = whole
             lines[4 + g, rows_here, :] = pltpu.roll(whole, 64, 1)
         return 0
 
-    lax.fori_loop(0, rows // 8, pack, 0)
+    lax.fori_loop(0, rows // 8, pack, 0, unroll=2)
 
     def place(r, _):
         slot = slot_of[r]

time: 108 us -> 106 us (0.981)
  Pallas kernels: 12.4 us -> 10.8 us
    pallas_call x1, Pallas kernels: 8.08 us -> 6.52 us  [local(): pl.pallas_call(source_kernel, out_shape=jax.ShapeDtypeStruct(whole, jnp.b...]
where the time goes in v6:
time: 106 us
  blocking collectives  95.4 us (90%)
  Pallas kernels  10.8 us (10%)
    all_to_all x1, blocking collectives, local(): got = lax.all_to_all(send.reshape(fine), ('lat', 'grp'), 0, 0, tiled=True)  95.4 us
    pallas_call x1, Pallas kernels, local(): pl.pallas_call(source_kernel, out_shape=jax.ShapeDtypeStruct(whole, jnp.b...  6.52 us
    pallas_call x1, Pallas kernels, local(): pl.pallas_call(tile_kernel, out_shape=jax.ShapeDtypeStruct((4, 4, 128, 12...  4.29 us

profile of v6, /device:TPU:1, one launch (start us, length us, event | category | flops | bytes accessed | tf_op | source)
XLA Modules:
  0.0 106.2 jit_solution(11558766959484806017)
XLA Ops:
  0.0 6.5 %lon_slots.1 = bf16[12800,128]{1,0:T(8,128)(2,1)} custom-call(s32[64]{0:T(128)} %bitcast.5, s32[64]{0:T(128)} %tile_hbm.1, s32[64]{0:T(128)} %offset_hbm.1, s32[64]{0:T(128)} %shift_hbm.1, f32[64]{0:T(128)} %lat_hbm.1, bf16[64,4,16,128]{3,2,1,0:T(8,128)(2,1)} %inc_hbm.1, f32[64,128]{1,0:T(8,128)} %lon_hbm.1), custom_call_target="tpu_custom_call" | custom-call | tf_op jit(solution)/shard_map/lon_slots/pallas_call | solution.py:251
  6.5 95.4 %all_to_all.5 = bf16[6400,2,128]{2,1,0:T(2,128)(2,1)S(1)} all-to-all(bf16[6400,2,128]{2,1,0:T(2,128)(2,1)} %bitcast.4), channel_id=1, replica_groups=mesh['lat'=64,'grp'=4] {'lat','grp'}, dimensions={0} | all-to-all | bytes 6553600 | tf_op jit(solution)/shard_map/all_to_all | solution.py:276
  102.0 4.3 %tile_sums.1 = f32[4,4,128,128]{3,2,1,0:T(8,128)} custom-call(bf16[12800,128]{1,0:T(8,128)(2,1)S(1)} %bitcast.3), custom_call_target="tpu_custom_call" | custom-call | tf_op jit(solution)/shard_map/tile_sums/pallas_call | solution.py:277

commit v7 on v6

--- a/solution.py
+++ b/solution.py
@@ -166,22 +166,22 @@
         wide[piece, :] = got[piece, :].astype(jnp.float32)
         return 0
 
-    lax.fori_loop(0, peers // 8, widen, 0)
+    lax.fori_loop(0, peers // 8, widen, 0, unroll=4)
 
     def line_of_all(row):
         return wide[pl.ds(row, peers, stride=PEER_ROWS), :]
 
     lanes = lax.broadcasted_iota(jnp.int32, (peers, 128), 1)
-    row_id = lanes.astype(jnp.float32)
     field, place = lanes // FIELD, lanes % FIELD
     pair_line = line_of_all(OWN_ROWS)
     slot_lines = [pair_line, pltpu.roll(pair_line, 64, 1), line_of_all(OWN_ROWS + 1)]
     stencil, here, over_next, over_own = [], [], [], []
     for line in slot_lines:
-        table = jnp.zeros((peers, 128), jnp.float32)
-        start = line[:, META : META + 1]
-        for k in range(4):
-            table = table + jnp.where(row_id == start + float(k), line[:, META + 2 + k : META + 3 + k], 0.0)
+        start = jnp.broadcast_to(line[:, META : META + 1], (peers, 128)).astype(jnp.int32)
+        offset = lanes - start
+        inside = (offset >= 0) & (offset < 4)
+        pick = jnp.where(inside, offset, 0) + (META + 2)
+        table = jnp.where(inside, jnp.take_along_axis(line, pick, axis=1), 0.0)
         stencil.append(table.T.astype(jnp.bfloat16))
         shift = jnp.broadcast_to(line[:, META + 1 : META + 2], (peers, 128)).astype(jnp.int32)
         step = lanes - shift

time: 106 us -> 106 us (level)
  no operation moved by 1% of the time
where the time goes in v7:
time: 106 us
  blocking collectives  95.4 us (90%)
  Pallas kernels  10.2 us (10%)
    all_to_all x1, blocking collectives, local(): got = lax.all_to_all(send.reshape(fine), ('lat', 'grp'), 0, 0, tiled=True)  95.4 us
    pallas_call x1, Pallas kernels, local(): pl.pallas_call(source_kernel, out_shape=jax.ShapeDtypeStruct(whole, jnp.b...  6.52 us
    pallas_call x1, Pallas kernels, local(): pl.pallas_call(tile_kernel, out_shape=jax.ShapeDtypeStruct((4, 4, 128, 12...  3.64 us

profile of v7, /device:TPU:1, one launch (start us, length us, event | category | flops | bytes accessed | tf_op | source)
XLA Modules:
  0.0 105.6 jit_solution(18443942971008493175)
XLA Ops:
  0.0 6.5 %lon_slots.1 = bf16[12800,128]{1,0:T(8,128)(2,1)} custom-call(s32[64]{0:T(128)} %bitcast.5, s32[64]{0:T(128)} %tile_hbm.1, s32[64]{0:T(128)} %offset_hbm.1, s32[64]{0:T(128)} %shift_hbm.1, f32[64]{0:T(128)} %lat_hbm.1, bf16[64,4,16,128]{3,2,1,0:T(8,128)(2,1)} %inc_hbm.1, f32[64,128]{1,0:T(8,128)} %lon_hbm.1), custom_call_target="tpu_custom_call" | custom-call | tf_op jit(solution)/shard_map/lon_slots/pallas_call | solution.py:251
  6.5 95.4 %all_to_all.5 = bf16[6400,2,128]{2,1,0:T(2,128)(2,1)S(1)} all-to-all(bf16[6400,2,128]{2,1,0:T(2,128)(2,1)} %bitcast.4), channel_id=1, replica_groups=mesh['lat'=64,'grp'=4] {'lat','grp'}, dimensions={0} | all-to-all | bytes 6553600 | tf_op jit(solution)/shard_map/all_to_all | solution.py:276
  102.0 3.6 %tile_sums.1 = f32[4,4,128,128]{3,2,1,0:T(8,128)} custom-call(bf16[12800,128]{1,0:T(8,128)(2,1)S(1)} %bitcast.3), custom_call_target="tpu_custom_call" | custom-call | tf_op jit(solution)/shard_map/tile_sums/pallas_call | solution.py:277

commit v8 on v7

--- a/solution.py
+++ b/solution.py
@@ -14,7 +14,6 @@
 META = OVER * SLOT_ROWS
 FIELD = 16
 PITCH = 65
-OUT_PARTS = 8
 SPARE = 72
 
 
@@ -34,7 +33,7 @@
 def source_kernel(
     band_hbm, tile_hbm, offset_hbm, shift_hbm, lat_hbm, inc_hbm, lon_hbm, out,
     band, tile_index, lat_offset, lon_shift, lat_frac, count, slot_of,
-    inc, lon_frac, weights, stage, packed, edges, meta_lines, lines, rests, sems, out_sems,
+    inc, lon_frac, weights, stage, edges, meta_lines, lines, rests, sems,
 ):
     rows = inc.shape[0]
     bands = count.shape[0]
@@ -106,7 +105,7 @@
         meta_lines[pl.ds(r, 1), :] = meta[0:1]
         return 0
 
-    lax.fori_loop(0, rows, one_row, 0, unroll=16)
+    lax.fori_loop(0, rows, one_row, 0, unroll=32)
 
     def pack(n, _):
         rows_here = pl.ds(pl.multiple_of(8 * n, 8), 8)
@@ -140,21 +139,12 @@
     stage[pl.ds(OWN_ROWS, 4 * bands, stride=PEER_ROWS), :] = rests[0] + rests[1]
     stage[pl.ds(OWN_ROWS + 1, 4 * bands, stride=PEER_ROWS), :] = rests[2]
 
-    size = out.shape[0] // OUT_PARTS
-    sends = []
-    for n in range(OUT_PARTS):
-
-        def finish(i, _):
-            piece = pl.ds(pl.multiple_of(n * size + i * part, 16), part)
-            packed[piece, :] = stage[piece, :].astype(jnp.bfloat16)
-            return 0
-
-        lax.fori_loop(0, bands // (2 * OUT_PARTS), finish, 0)
-        span = pl.ds(n * size, size)
-        sends.append(pltpu.make_async_copy(packed.at[span, :], out.at[span, :], out_sems.at[n]))
-        sends[-1].start()
-    for send in sends:
-        send.wait()
+    def finish(i, _):
+        piece = pl.ds(pl.multiple_of(i * part, 16), part)
+        out[piece, :] = stage[piece, :].astype(jnp.bfloat16)
+        return 0
+
+    lax.fori_loop(0, bands // 2, finish, 0)
 
 
 def tile_kernel(got, out, wide, result, sems):
@@ -248,11 +238,12 @@
     vmem = pl.BlockSpec(memory_space=pltpu.VMEM)
     whole = (peers * PEER_ROWS, 128)
     roomy = (peers * PEER_ROWS + SPARE, 128)
+    operands = (band.reshape(rows), tile_index, lat_offset, lon_shift, lat_frac, increments, lon_frac)
     send = pl.pallas_call(
         source_kernel,
         out_shape=jax.ShapeDtypeStruct(whole, jnp.bfloat16),
         in_specs=[hbm] * 7,
-        out_specs=hbm,
+        out_specs=vmem,
         scratch_shapes=[pltpu.SMEM((rows,), jnp.int32)] * 4
         + [pltpu.SMEM((rows,), jnp.float32), pltpu.SMEM((n_lat,), jnp.int32)]
         + [pltpu.SMEM((rows,), jnp.int32)]
@@ -261,17 +252,15 @@
             pltpu.VMEM((rows, 128), jnp.float32),
             pltpu.VMEM((4, rows, 128), jnp.float32),
             pltpu.VMEM(roomy, jnp.float32),
-            pltpu.VMEM(whole, jnp.bfloat16),
             pltpu.VMEM((rows * PITCH + SPARE, 128), jnp.float32),
             pltpu.VMEM((rows, 128), jnp.float32),
             pltpu.VMEM((8, rows, 128), jnp.float32),
             pltpu.VMEM((CAP, peers, 128), jnp.float32),
             pltpu.SemaphoreType.DMA((7,)),
-            pltpu.SemaphoreType.DMA((OUT_PARTS,)),
         ],
-        compiler_params=pltpu.CompilerParams(vmem_limit_bytes=60 << 20),
+        compiler_params=pltpu.CompilerParams(vmem_limit_bytes=32 << 20),
         name="lon_slots",
-    )(band.reshape(rows), tile_index, lat_offset, lon_shift, lat_frac, increments, lon_frac)
+    )(*[pltpu.with_memory_space_constraint(operand, pltpu.HBM) for operand in operands])
     fine = (peers * PEER_ROWS // 2, 2, 128)
     got = lax.all_to_all(send.reshape(fine), ("lat", "grp"), 0, 0, tiled=True)
     return pl.pallas_call(

time: 106 us -> 104 us (0.981)
  Pallas kernels: 10.2 us -> 8.7 us
    pallas_call x1, Pallas kernels: 6.52 us -> 5.06 us  [local(): pl.pallas_call(source_kernel, out_shape=jax.ShapeDtypeStruct(whole, jnp.b...]
where the time goes in v8:
time: 104 us
  blocking collectives  95.2 us (92%)
  Pallas kernels  8.7 us (8%)
    all_to_all x1, blocking collectives, local(): got = lax.all_to_all(send.reshape(fine), ('lat', 'grp'), 0, 0, tiled=True)  95.2 us
    pallas_call x1, Pallas kernels, local(): pl.pallas_call(source_kernel, out_shape=jax.ShapeDtypeStruct(whole, jnp.b...  5.06 us
    pallas_call x1, Pallas kernels, local(): pl.pallas_call(tile_kernel, out_shape=jax.ShapeDtypeStruct((4, 4, 128, 12...  3.64 us

profile of v8, /device:TPU:1, one launch (start us, length us, event | category | flops | bytes accessed | tf_op | source)
XLA Modules:
  0.0 103.9 jit_solution(15635466409617435456)
XLA Ops:
  0.0 5.1 %lon_slots.1 = bf16[12800,128]{1,0:T(8,128)(2,1)S(1)} custom-call(s32[64]{0:T(128)} %bitcast.5, s32[64]{0:T(128)} %tile_hbm.1, s32[64]{0:T(128)} %offset_hbm.1, s32[64]{0:T(128)} %shift_hbm.1, f32[64]{0:T(128)} %lat_hbm.1, bf16[64,4,16,128]{3,2,1,0:T(8,128)(2,1)} %inc_hbm.1, f32[64,128]{1,0:T(8,128)} %lon_hbm.1), custom_call_target="tpu_custom_call" | custom-call | tf_op jit(solution)/shard_map/lon_slots/pallas_call | solution.py:242
  5.1 95.2 %all_to_all.5 = bf16[6400,2,128]{2,1,0:T(2,128)(2,1)S(1)} all-to-all(bf16[6400,2,128]{2,1,0:T(2,128)(2,1)S(1)} %bitcast.4), channel_id=1, replica_groups=mesh['lat'=64,'grp'=4] {'lat','grp'}, dimensions={0} | all-to-all | bytes 6553600 | tf_op jit(solution)/shard_map/all_to_all | solution.py:265
  100.3 3.6 %tile_sums.1 = f32[4,4,128,128]{3,2,1,0:T(8,128)} custom-call(bf16[12800,128]{1,0:T(8,128)(2,1)S(1)} %bitcast.3), custom_call_target="tpu_custom_call" | custom-call | tf_op jit(solution)/shard_map/tile_sums/pallas_call | solution.py:266

commit v9 on v8

--- a/solution.py
+++ b/solution.py
@@ -41,7 +41,11 @@
         (band_hbm, band), (tile_hbm, tile_index), (offset_hbm, lat_offset), (shift_hbm, lon_shift),
         (lat_hbm, lat_frac),
     )
-    pairs = ((inc_hbm, inc), (lon_hbm, lon_frac)) + pairs
+    near = rows // 2
+    pairs = (
+        (inc_hbm.at[pl.ds(0, near)], inc.at[pl.ds(0, near)]), (lon_hbm, lon_frac),
+        (inc_hbm.at[pl.ds(near, rows - near)], inc.at[pl.ds(near, rows - near)]),
+    ) + pairs
     copies = [pltpu.make_async_copy(src, dst, sems.at[i]) for i, (src, dst) in enumerate(pairs)]
     for copy in copies:
         copy.start()
@@ -57,14 +61,14 @@
         count[2 * i + 1] = 0
         return 0
 
-    lax.fori_loop(0, bands // 2, clear, 0)
+    lax.fori_loop(0, bands // 2, clear, 0, unroll=4)
     rests[...] = jnp.zeros(rests.shape, jnp.float32)
     copies[1].wait()
 
     for m, w in enumerate(lagrange(lon_frac[...])):
         weights[m] = rounded(w)
 
-    for copy in copies[2:]:
+    for copy in copies[3:]:
         copy.wait()
     copies[0].wait()
 
@@ -105,7 +109,9 @@
         meta_lines[pl.ds(r, 1), :] = meta[0:1]
         return 0
 
-    lax.fori_loop(0, rows, one_row, 0, unroll=32)
+    lax.fori_loop(0, near, one_row, 0, unroll=32)
+    copies[2].wait()
+    lax.fori_loop(near, rows, one_row, 0, unroll=32)
 
     def pack(n, _):
         rows_here = pl.ds(pl.multiple_of(8 * n, 8), 8)
@@ -144,7 +150,7 @@
         out[piece, :] = stage[piece, :].astype(jnp.bfloat16)
         return 0
 
-    lax.fori_loop(0, bands // 2, finish, 0)
+    lax.fori_loop(0, bands // 2, finish, 0, unroll=4)
 
 
 def tile_kernel(got, out, wide, result, sems):
@@ -156,7 +162,7 @@
         wide[piece, :] = got[piece, :].astype(jnp.float32)
         return 0
 
-    lax.fori_loop(0, peers // 8, widen, 0, unroll=4)
+    lax.fori_loop(0, peers // 8, widen, 0, unroll=8)
 
     def line_of_all(row):
         return wide[pl.ds(row, peers, stride=PEER_ROWS), :]
@@ -256,7 +262,7 @@
             pltpu.VMEM((rows, 128), jnp.float32),
             pltpu.VMEM((8, rows, 128), jnp.float32),
             pltpu.VMEM((CAP, peers, 128), jnp.float32),
-            pltpu.SemaphoreType.DMA((7,)),
+            pltpu.SemaphoreType.DMA((8,)),
         ],
         compiler_params=pltpu.CompilerParams(vmem_limit_bytes=32 << 20),
         name="lon_slots",

time: 104 us -> 104 us (level)
  no operation moved by 1% of the time
where the time goes in v9:
time: 104 us
  blocking collectives  95.2 us (92%)
  Pallas kernels  8.44 us (8%)
    all_to_all x1, blocking collectives, local(): got = lax.all_to_all(send.reshape(fine), ('lat', 'grp'), 0, 0, tiled=True)  95.2 us
    pallas_call x1, Pallas kernels, local(): pl.pallas_call(source_kernel, out_shape=jax.ShapeDtypeStruct(whole, jnp.b...  4.82 us
    pallas_call x1, Pallas kernels, local(): pl.pallas_call(tile_kernel, out_shape=jax.ShapeDtypeStruct((4, 4, 128, 12...  3.63 us

profile of v9, /device:TPU:1, one launch (start us, length us, event | category | flops | bytes accessed | tf_op | source)
XLA Modules:
  0.0 103.7 jit_solution(2676789240202370262)
XLA Ops:
  0.0 4.8 %lon_slots.1 = bf16[12800,128]{1,0:T(8,128)(2,1)S(1)} custom-call(s32[64]{0:T(128)} %bitcast.5, s32[64]{0:T(128)} %tile_hbm.1, s32[64]{0:T(128)} %offset_hbm.1, s32[64]{0:T(128)} %shift_hbm.1, f32[64]{0:T(128)} %lat_hbm.1, bf16[64,4,16,128]{3,2,1,0:T(8,128)(2,1)} %inc_hbm.1, f32[64,128]{1,0:T(8,128)} %lon_hbm.1), custom_call_target="tpu_custom_call" | custom-call | tf_op jit(solution)/shard_map/lon_slots/pallas_call | solution.py:248
  4.8 95.2 %all_to_all.5 = bf16[6400,2,128]{2,1,0:T(2,128)(2,1)S(1)} all-to-all(bf16[6400,2,128]{2,1,0:T(2,128)(2,1)S(1)} %bitcast.4), channel_id=1, replica_groups=mesh['lat'=64,'grp'=4] {'lat','grp'}, dimensions={0} | all-to-all | bytes 6553600 | tf_op jit(solution)/shard_map/all_to_all | solution.py:271
  100.0 3.6 %tile_sums.1 = f32[4,4,128,128]{3,2,1,0:T(8,128)} custom-call(bf16[12800,128]{1,0:T(8,128)(2,1)S(1)} %bitcast.3), custom_call_target="tpu_custom_call" | custom-call | tf_op jit(solution)/shard_map/tile_sums/pallas_call | solution.py:272
